TPU v7x, 512 devices: a whole 4x8x8 slice. The times are simulated.
512 devices in a mesh: rep: 8 (over z), kv: 64 (over x, y, core).
Axes of the slice: x: 4, y: 8, z: 8, core: 2. Of those that a mesh axis runs over, the one named last changes fastest.
Arguments:
- queries: bfloat16 [64, 64, 576], P('rep'), parts along dimension 0, may hold values from -400 to 400
- latent_cache: bfloat16 [64, 16384, 576], P('rep', 'kv'), parts along dimension 0, may hold values from -6.1 to 6.1
- lengths: int32 [64], P('rep'), parts along dimension 0, may hold values from 8192 to 16384, as said below
- value_up: bfloat16 [64, 512, 128], P('kv'), may hold values from -1 to 1
- out_proj: bfloat16 [8192, 7168], P('kv'), may hold values from -0.1875 to 0.1875
Outputs:
- attended: bfloat16 [64, 7168], P('rep', 'kv'), parts along dimension 0
There are 8 independent parts, one for each index of `rep`. A program takes and returns all parts, laid end to end along the dimension named above; an argument that names none is the same for every part. Nothing has to cross between parts.
Inputs may be any that keep to these rules, and one draw needn't show every extreme that they name: `lengths`: some request has length 16384.
All inputs are finite; a program needn't handle non-finite values.
Results may differ from a plain program's by a relative error of at most 0.02.
Values sent between devices are 32-bit elements; how exact they have to be, the bound alone decides.
No kernel may reach another device: no remote copies, remote signals or barrier semaphores. Data moves between devices by JAX's collectives and lax.ppermute only.
A program may use at most 64 MiB of HBM per device.

v0:
```python
import jax
import jax.numpy as jnp
from jax import lax
from jax.sharding import PartitionSpec as P

LATENT = 512


softmax_scale = 192.0 ** (-0.5)
masked_value = -1e30


def merge_sources(source_out, source_max, source_sum):
    global_max = jnp.max(source_max, axis=0)
    scaled = source_sum * jnp.exp(source_max - global_max[None])
    coefficient = scaled / jnp.sum(scaled, axis=0)[None]
    return jnp.sum(coefficient[..., None] * source_out, axis=0).astype(jnp.bfloat16)


def on_device(queries, latent_cache, lengths, value_up, out_proj):
    shard_len = latent_cache.shape[1]
    offset = lax.axis_index("kv") * shard_len
    positions = offset + jnp.arange(shard_len, dtype=jnp.int32)
    live_mask = positions[None, :] < lengths[:, None]
    scores = (
        jnp.einsum("rhk,rsk->rhs", queries, latent_cache, preferred_element_type=jnp.float32)
        * softmax_scale
    )
    scores = jnp.where(live_mask[:, None, :], scores, masked_value)
    maxima = jnp.max(scores, axis=-1)
    exponents = jnp.where(live_mask[:, None, :], jnp.exp(scores - maxima[..., None]), 0.0)
    totals = jnp.sum(exponents, axis=-1)
    numerators = jnp.einsum(
        "rhs,rsl->rhl",
        exponents.astype(jnp.bfloat16),
        latent_cache[:, :, :LATENT],
        preferred_element_type=jnp.float32,
    )
    partial_out = (numerators / jnp.maximum(totals, 1.0)[..., None]).astype(jnp.bfloat16)
    partial_wide = partial_out.astype(jnp.float32)
    combined = merge_sources(
        lax.all_to_all(partial_wide[None], "kv", split_axis=2, concat_axis=0, tiled=True),
        lax.all_to_all(maxima[None], "kv", split_axis=2, concat_axis=0, tiled=True),
        lax.all_to_all(totals[None], "kv", split_axis=2, concat_axis=0, tiled=True),
    )
    head_values = jnp.einsum("rhl,hlv->rhv", combined, value_up, preferred_element_type=jnp.float32)
    flat_values = head_values.astype(jnp.bfloat16).reshape(combined.shape[0], -1)
    projection = jnp.dot(flat_values, out_proj, preferred_element_type=jnp.float32)
    return lax.psum_scatter(projection, "kv", scatter_dimension=1, tiled=True).astype(jnp.bfloat16)


def solution(mesh):
    placed = (
        P("rep", None, None),
        P("rep", "kv", None),
        P("rep"),
        P("kv", None, None),
        P("kv", None),
    )
    return jax.shard_map(
        on_device, mesh=mesh, in_specs=placed, out_specs=P("rep", "kv"), check_vma=False
    )
```

profile of v0, /device:TPU:1, one launch (start us, length us, event | category | flops | bytes accessed | tf_op | source)
XLA Modules:
  0.0 236.8 jit_solution(15576381589175232978)
XLA Ops:
  6.5 0.0 copy-start
  6.5 0.9 broadcast_compare_fusion
  7.4 2.5 %fusion.30 = (f32[8,64]{1,0:T(8,128)S(1)}, f32[8,64,256]{2,1,0:T(8,128)S(1)}) fusion(bf16[8,64,576]{2,1,0:T(8,128)(2,1)} %param.5, bf16[8,256,576]{1,2,0:T(8,128)(2,1)} %param.6, pred[8,256]{1,0:T(8,128)(4,1)S(1)} %broadcast_compare_fusion), kind=kOutput, calls=%fused_computation.29 | convolution fusion | flops 151387648 | bytes 3477504 | tf_op jit(solution)/shard_map/rhk,rsk->rhs/dot_general | solution.py:26
  9.9 0.3 fusion.17
  10.2 0.7 copy.11
  10.9 11.6 %all-to-all-start = ((f32[1,8,64]{1,0,2:T(1,128)}), f32[1,8,64]{1,0,2:T(1,128)S(1)}, u32[]{:S(2)}, u32[]{:S(2)}) async-start(f32[1,8,64]{1,0,2:T(1,128)} %copy.11), calls=%async_computation | async-start | bytes 65536 | tf_op jit(solution)/shard_map/all_to_all | solution.py:44
  22.5 0.7 copy.12
  23.2 8.6 %all-to-all-done = f32[1,8,64]{1,0,2:T(1,128)S(1)} async-done(((f32[1,8,64]{1,0,2:T(1,128)}), f32[1,8,64]{1,0,2:T(1,128)S(1)}, u32[]{:S(2)}, u32[]{:S(2)}) %all-to-all-start) | async-done | bytes 2080 | tf_op jit(solution)/shard_map/all_to_all | solution.py:44
  31.8 4.7 %all-to-all-start.1 = ((f32[1,8,64]{1,0,2:T(1,128)}), f32[1,8,64]{1,0,2:T(1,128)S(1)}, u32[]{:S(2)}, u32[]{:S(2)}) async-start(f32[1,8,64]{1,0,2:T(1,128)} %copy.12), calls=%async_computation.1 | async-start | bytes 65536 | tf_op jit(solution)/shard_map/all_to_all | solution.py:43
  36.5 2.4 fusion.12
  38.9 0.0 copy-start.1
  38.9 1.6 copy.14
  40.5 5.4 %all-to-all-done.1 = f32[1,8,64]{1,0,2:T(1,128)S(1)} async-done(((f32[1,8,64]{1,0,2:T(1,128)}), f32[1,8,64]{1,0,2:T(1,128)S(1)}, u32[]{:S(2)}, u32[]{:S(2)}) %all-to-all-start.1) | async-done | bytes 2080 | tf_op jit(solution)/shard_map/all_to_all | solution.py:43
  45.9 5.0 %all-to-all-start.2 = ((f32[1,8,64,512]{3,1,0,2:T(8,128)}), f32[1,8,64,512]{3,1,0,2:T(8,128)S(1)}, u32[]{:S(2)}, u32[]{:S(2)}) async-start(f32[1,8,64,512]{3,1,0,2:T(8,128)} %copy.14), calls=%async_computation.2 | async-start | bytes 2097152 | tf_op jit(solution)/shard_map/all_to_all | solution.py:42
  50.9 0.0 reduce-scatter.4.cloned.1.call-start
  51.0 0.1 reduce_max.19
  51.1 28.4 %all-to-all-done.2 = f32[1,8,64,512]{3,1,0,2:T(8,128)S(1)} async-done(((f32[1,8,64,512]{3,1,0,2:T(8,128)}), f32[1,8,64,512]{3,1,0,2:T(8,128)S(1)}, u32[]{:S(2)}, u32[]{:S(2)}) %all-to-all-start.2) | async-done | bytes 1048608 | tf_op jit(solution)/shard_map/all_to_all | solution.py:42
  79.5 0.1 fusion.15
  79.6 0.0 copy-done
  79.6 0.0 copy-done.1
  79.6 2.6 %convolution_bitcast_fusion = f32[7168,8]{1,0:T(8,128)} fusion(bf16[128,7168]{1,0:T(8,128)(2,1)S(1)} %copy-done, bf16[1,512,128]{2,1,0:T(8,128)(2,1)S(1)} %copy-done.1, bf16[8,512]{1,0:T(8,128)(2,1)S(1)} %fusion.15), kind=kOutput, calls=%fused_computation | convolution fusion | flops 15729664 | bytes 2203648
  82.3 0.0 reduce-scatter.4.cloned.1.call-update
  82.3 146.2 %reduce-scatter.4.cloned.1.call-done = f32[112,8]{1,0:T(8,128)} async-done(((f32[7168,8]{1,0:T(8,128)}), f32[112,8]{1,0:T(8,128)}) %reduce-scatter.4.cloned.1.call-update) | async-done | bytes 3600
  228.5 1.5 copy.16
  (4 shorter events, 0.1 us)
Async XLA Ops:
  6.5 73.1 %copy-start = (bf16[128,7168]{1,0:T(8,128)(2,1)S(1)}, bf16[128,7168]{1,0:T(8,128)(2,1)}, u32[]{:S(2)}) copy-start(bf16[128,7168]{1,0:T(8,128)(2,1)} %param.9) | copy-start | bytes 5505028
  10.9 20.9 %all-to-all-start = ((f32[1,8,64]{1,0,2:T(1,128)}), f32[1,8,64]{1,0,2:T(1,128)S(1)}, u32[]{:S(2)}, u32[]{:S(2)}) async-start(f32[1,8,64]{1,0,2:T(1,128)} %copy.11), calls=%async_computation | async-start | bytes 65536 | tf_op jit(solution)/shard_map/all_to_all | solution.py:44
  31.8 14.1 %all-to-all-start.1 = ((f32[1,8,64]{1,0,2:T(1,128)}), f32[1,8,64]{1,0,2:T(1,128)S(1)}, u32[]{:S(2)}, u32[]{:S(2)}) async-start(f32[1,8,64]{1,0,2:T(1,128)} %copy.12), calls=%async_computation.1 | async-start | bytes 65536 | tf_op jit(solution)/shard_map/all_to_all | solution.py:43
  38.9 40.8 %copy-start.1 = (bf16[1,512,128]{2,1,0:T(8,128)(2,1)S(1)}, bf16[1,512,128]{2,1,0:T(8,128)(2,1)}, u32[]{:S(2)}) copy-start(bf16[1,512,128]{2,1,0:T(8,128)(2,1)} %param.8) | copy-start | bytes 393220
  45.9 33.6 %all-to-all-start.2 = ((f32[1,8,64,512]{3,1,0,2:T(8,128)}), f32[1,8,64,512]{3,1,0,2:T(8,128)S(1)}, u32[]{:S(2)}, u32[]{:S(2)}) async-start(f32[1,8,64,512]{3,1,0,2:T(8,128)} %copy.14), calls=%async_computation.2 | async-start | bytes 2097152 | tf_op jit(solution)/shard_map/all_to_all | solution.py:42
  50.9 177.6 %reduce-scatter.4.cloned.1.call-start = ((), (), s32[]{:S(2)}) async-start(), calls=%async_computation.4 | async-start | bytes 3727360
Sparse Core Ops, SparseCore 0:
  82.4 146.0 reduce-scatter.3
where the time goes:
time: 241 us; the launch traced here: 237 us
  waiting for transfers between devices  189 us (78%)
  starting transfers between devices  21.4 us (9%)
  between operations  13.5 us (6%)
  matrix products  7.52 us (3%)
  local copies, waits for them, and re-layouts  4.44 us (2%)
    unnamed x2, waiting for transfers between devices  146 us
    all_to_all x1, waiting for transfers between devices, on_device(): lax.all_to_all(partial_wide[None], 'kv', split_axis=2, concat_axis=0, til...  28.4 us
    all_to_all x1, starting transfers between devices, on_device(): lax.all_to_all(totals[None], 'kv', split_axis=2, concat_axis=0, tiled=True)  11.6 us
    all_to_all x1, waiting for transfers between devices, on_device(): lax.all_to_all(totals[None], 'kv', split_axis=2, concat_axis=0, tiled=True)  8.59 us
    all_to_all x1, waiting for transfers between devices, on_device(): lax.all_to_all(maxima[None], 'kv', split_axis=2, concat_axis=0, tiled=True)  5.42 us
    all_to_all x1, starting transfers between devices, on_device(): lax.all_to_all(partial_wide[None], 'kv', split_axis=2, concat_axis=0, til...  5.01 us
  transfers between devices with their start and end apart: 4, of which 4 were waited for; matrix products, arithmetic and copies ran while one was open for 2% of the time, Pallas kernels for 0%

commit v1 on v0

v1 whole, which is shorter than its diff:
```python
import jax
import jax.numpy as jnp
from jax import lax
from jax.sharding import PartitionSpec as P

LATENT = 512


softmax_scale = 192.0 ** (-0.5)
masked_value = -1e30


def core_swap(x, kv):
    return lax.ppermute(x, "kv", [(i, i ^ 1) for i in range(kv)])


def merge_two(a, b):
    top = jnp.maximum(a[..., LATENT : LATENT + 1], b[..., LATENT : LATENT + 1])
    lane = lax.broadcasted_iota(jnp.int32, a.shape, a.ndim - 1)
    wa = jnp.where(lane == LATENT, 1.0, jnp.exp(a[..., LATENT : LATENT + 1] - top))
    wb = jnp.exp(b[..., LATENT : LATENT + 1] - top)
    return jnp.where(lane == LATENT, top, a * wa + b * wb)


def on_device(kv, queries, latent_cache, lengths, value_up, out_proj):
    rows, shard_len = latent_cache.shape[:2]
    heads = queries.shape[1]
    me = lax.axis_index("kv")
    core = lax.rem(me, 2)
    offset = me * shard_len
    positions = offset + jnp.arange(shard_len, dtype=jnp.int32)
    live_mask = positions[None, :] < lengths[:, None]
    scores = (
        jnp.einsum("rhk,rsk->rhs", queries, latent_cache, preferred_element_type=jnp.float32)
        * softmax_scale
    )
    scores = jnp.where(live_mask[:, None, :], scores, masked_value)
    maxima = jnp.max(scores, axis=-1)
    exponents = jnp.where(live_mask[:, None, :], jnp.exp(scores - maxima[..., None]), 0.0)
    totals = jnp.sum(exponents, axis=-1)
    numerators = jnp.einsum(
        "rhs,rsl->rhl",
        exponents.astype(jnp.bfloat16),
        latent_cache[:, :, :LATENT],
        preferred_element_type=jnp.float32,
    )
    stats = jnp.stack([maxima, totals], axis=-1)
    packed = jnp.concatenate([numerators, jnp.pad(stats, ((0, 0), (0, 0), (0, 126)))], axis=-1)
    packed = packed.reshape(rows, heads // 2, 2, LATENT + 128).transpose(2, 1, 0, 3)
    mine = lax.dynamic_index_in_dim(packed, core, 0, keepdims=False)
    theirs = lax.dynamic_index_in_dim(packed, 1 - core, 0, keepdims=False)
    pair = merge_two(mine, core_swap(theirs, kv))
    chips = [[2 * i + c for i in range(kv // 2)] for c in range(2)]
    got = lax.all_to_all(pair, "kv", 0, 0, axis_index_groups=chips)
    top = got[..., LATENT]
    weight = jnp.exp(top - jnp.max(top, axis=0)[None])
    total = jnp.sum(weight * got[..., LATENT + 1], axis=0)
    combined = jnp.sum(weight[..., None] * got[..., :LATENT], axis=0) / total[..., None]
    head_values = jnp.dot(
        combined.astype(jnp.bfloat16), value_up[0], preferred_element_type=jnp.float32
    )
    projection = jnp.dot(
        head_values.astype(jnp.bfloat16), out_proj, preferred_element_type=jnp.float32
    )
    features = out_proj.shape[1] // kv
    blocks = projection.reshape(rows, kv // 2, 2, features).transpose(2, 1, 0, 3)
    mine = lax.dynamic_index_in_dim(blocks, core, 0, keepdims=False)
    theirs = lax.dynamic_index_in_dim(blocks, 1 - core, 0, keepdims=False)
    summed = mine + core_swap(theirs, kv)
    parts = lax.all_to_all(summed, "kv", 0, 0, axis_index_groups=chips)
    return jnp.sum(parts, axis=0).astype(jnp.bfloat16)


def solution(mesh):
    kv = mesh.shape["kv"]
    placed = (
        P("rep", None, None),
        P("rep", "kv", None),
        P("rep"),
        P("kv", None, None),
        P("kv", None),
    )

    def device_step(*args):
        return on_device(kv, *args)

    return jax.shard_map(
        device_step, mesh=mesh, in_specs=placed, out_specs=P("rep", "kv"), check_vma=False
    )
```

time: 241 us -> 80 us (0.33); the launches traced: 237 us -> 79 us
  waiting for transfers between devices: 189 us -> 0.97 us
  blocking collectives: 0 us -> 36.1 us
  between operations: 13.5 us -> 0.16 us
  local copies, waits for them, and re-layouts: 4.44 us -> 14.2 us
  other arithmetic: 1.41 us -> 10.1 us
  starting transfers between devices: 21.4 us -> 13.6 us
  matrix products: 7.52 us -> 3.87 us
    unnamed x2 -> x0, waiting for transfers between devices: 146 us -> none
    all_to_all x3 -> x0, waiting for transfers between devices: 42.4 us -> none  [the longest x1 28.4 us: on_device(): lax.all_to_all(partial_wide[None], 'kv', split_axis=2, concat_axis=0, til...]
    all_to_all x0 -> x2, blocking collectives: none -> 36.1 us  [the longest x1 21.6 us: on_device(): got = lax.all_to_all(pair, 'kv', 0, 0, axis_index_groups=chips)]
    all_to_all x3 -> x0, starting transfers between devices: 21.3 us -> none  [the longest x1 11.6 us: on_device(): lax.all_to_all(totals[None], 'kv', split_axis=2, concat_axis=0, tiled=True)]
    ppermute x0 -> x2, starting transfers between devices: none -> 13.6 us  [core_swap(): return lax.ppermute(x, 'kv', [(i, i ^ 1) for i in range(kv)])]
    select_n x0 -> x1, other arithmetic: none -> 5.77 us  [merge_two(): return jnp.where(lane == LATENT, top, a * wa + b * wb)]
    broadcast_in_dim x3 -> x0, local copies, waits for them, and re-layouts: 2.97 us -> none  [the longest x1 1.6 us: on_device(): partial_wide[None]]
    unnamed x5 -> x12, local copies, waits for them, and re-layouts: 1.47 us -> 4.37 us
  transfers between devices with their start and end apart: 4 -> 2, of which waited for: 4 -> 1; matrix products, arithmetic and copies ran while one was open for 2% -> 4% of each run, Pallas kernels for 0% -> 0%
where the time goes in v1:
time: 80 us; the launch traced here: 79 us
  blocking collectives  36.1 us (45%)
  local copies, waits for them, and re-layouts  14.2 us (18%)
  starting transfers between devices  13.6 us (17%)
  other arithmetic  10.1 us (13%)
  matrix products  3.87 us (5%)
  waiting for transfers between devices  0.97 us (1%)
    all_to_all x1, blocking collectives, on_device(): got = lax.all_to_all(pair, 'kv', 0, 0, axis_index_groups=chips)  21.6 us
    all_to_all x1, blocking collectives, on_device(): parts = lax.all_to_all(summed, 'kv', 0, 0, axis_index_groups=chips)  14.5 us
    ppermute x2, starting transfers between devices, core_swap(): return lax.ppermute(x, 'kv', [(i, i ^ 1) for i in range(kv)])  13.6 us
    select_n x1, other arithmetic, merge_two(): return jnp.where(lane == LATENT, top, a * wa + b * wb)  5.77 us
    unnamed x12, local copies, waits for them, and re-layouts  4.37 us
    dot_general x1, matrix products, on_device(): jnp.einsum('rhk,rsk->rhs', queries, latent_cache, preferred_element_type=...  2.6 us
    select_n x1, local copies, waits for them, and re-layouts, merge_two(): return jnp.where(lane == LATENT, top, a * wa + b * wb)  2.44 us
    another operation x2, local copies, waits for them, and re-layouts  2.4 us
  transfers between devices with their start and end apart: 2, of which 1 were waited for; matrix products, arithmetic and copies ran while one was open for 4% of the time, Pallas kernels for 0%

profile of v1, /device:TPU:1, one launch (start us, length us, event | category | flops | bytes accessed | tf_op | source)
XLA Modules:
  0.0 79.0 jit_solution(6689535748760822073)
XLA Ops:
  0.0 0.0 copy-start
  0.0 0.0 copy-start.1
  0.0 0.9 %broadcast_compare_fusion = pred[8,256]{1,0:T(8,128)(4,1)S(1)} fusion(s32[256]{0:T(256)S(1)} %iota_add_fusion, s32[8]{0:T(128)} %param.7), kind=kLoop, calls=%fused_computation.32 | loop fusion | flops 2048 | bytes 3104 | tf_op jit(solution)/shard_map/lt | solution.py:32
  0.9 2.6 %fusion.21 = (f32[8,64]{1,0:T(8,128)S(1)}, f32[8,64,256]{2,1,0:T(8,128)S(1)}) fusion(bf16[8,64,576]{2,1,0:T(8,128)(2,1)} %param.5, bf16[8,256,576]{1,2,0:T(8,128)(2,1)} %param.6, pred[8,256]{1,0:T(8,128)(4,1)S(1)} %broadcast_compare_fusion), kind=kOutput, calls=%fused_computation.44 | convolution fusion | flops 151387648 | bytes 3477504 | tf_op jit(solution)/shard_map/rhk,rsk->rhs/dot_general | solution.py:34
  3.5 0.3 fusion.5
  3.8 0.0 copy-done.1
  3.8 0.8 fusion
  4.6 0.1 copy.17
  4.7 1.2 %select_maximum_fusion = f32[8,64,640]{2,1,0:T(8,128)} fusion(f32[8,64,2]{2,1,0:T(8,128)S(1)} %copy.17, f32[8,64,512]{2,1,0:T(8,128)S(1)} %fusion), kind=kLoop, calls=%fused_computation.3 | loop fusion | flops 983040 | bytes 2363392 | tf_op jit(solution)/shard_map/concatenate | solution.py:48
  5.9 2.1 %reshape.41 = f32[8,32,2,640]{3,2,1,0:T(2,128)S(1)} reshape(f32[8,64,640]{2,1,0:T(8,128)} %select_maximum_fusion) | data formatting | bytes 2621440 | tf_op jit(solution)/shard_map/reshape | solution.py:49
  8.0 2.1 %constant_dynamic-slice_fusion.3 = (f32[8,32,1,640]{3,2,1,0:T(1,128)}, f32[8,32,1,640]{3,2,1,0:T(1,128)S(1)}) fusion(f32[8,32,2,640]{3,2,1,0:T(2,128)S(1)} %reshape.41, s32[]{:T(128)S(6)} %select_n.27, s32[]{:T(128)S(6)} %select_n.28), kind=kLoop, calls=%fused_computation.38 | loop fusion | bytes 2621448 | tf_op jit(solution)/shard_map/dynamic-slice
  10.1 0.4 copy.43
  10.5 8.8 %collective-permute-start = (f32[32,8,640]{2,1,0:T(8,128)S(1)}, f32[32,8,640]{2,1,0:T(8,128)S(1)}, u32[]{:S(2)}, u32[]{:S(2)}) collective-permute-start(f32[32,8,640]{2,1,0:T(8,128)S(1)} %bitcast.48), channel_id=1, source_target_pairs={{0,1},{1,0},{2,3},{3,2},{4,5},{5,4},{6,7},{7,6},{8,9},{9,8},{10,11... | collective-permute-start | bytes 1966088 | tf_op jit(solution)/shard_map/ppermute | solution.py:14
  19.3 3.5 %copy.31 = f32[8,32,1,640]{1,0,3,2:T(8,128)} copy(f32[8,32,1,640]{3,2,1,0:T(1,128)} %get-tuple-element.8) | data formatting | bytes 1310720
  22.8 0.0 collective-permute-done
  22.8 2.1 %copy.20 = f32[32,8,640]{0,1,2:T(8,128)} copy(f32[32,8,640]{2,1,0:T(8,128)S(1)} %collective-permute-done) | data formatting | bytes 1310720 | tf_op jit(solution)/shard_map/ppermute | solution.py:14
  24.9 0.7 fusion.19
  25.6 5.8 %add_select_fusion = f32[32,8,640]{0,1,2:T(8,128)} fusion(f32[32,8,640]{0,1,2:T(8,128)} %copy.20, f32[32,8]{0,1:T(8,128)S(1)} %get-tuple-element.7, f32[32,8]{0,1:T(8,128)S(1)} %get-tuple-element.6, f32[32,8]{0,1:T(8,128)S(1)} %get-tuple-element.5, pred[640]{0:T(1024)(128)(4,1)S(1)} %iota_compare_fusion.1, f32[8,32,1,640]{1,0,3,2:T(8,128)} %copy.31), kind=kLoop, calls=%fused_computation | loop fusion | flops 819200 | bytes 1969792 | tf_op jit(solution)/shard_map/jit(_where)/select_n | solution.py:22
  31.4 0.0 copy-start.2
  31.4 2.4 %copy.22 = f32[32,8,640]{2,1,0:T(8,128)S(1)} copy(f32[32,8,640]{0,1,2:T(8,128)} %add_select_fusion) | data formatting | bytes 1310720 | tf_op jit(solution)/shard_map/jit(_where)/select_n | solution.py:22
  33.8 21.6 %all_to_all.10 = f32[32,8,640]{2,1,0:T(8,128)S(1)} all-to-all(f32[32,8,640]{2,1,0:T(8,128)S(1)} %copy.22), channel_id=1, replica_groups={{0,2,4,6,8,10,12,14,16,18,20,22,24,26,28,30,32,34,36,38,40,42,44,46,48,..., dimensions={0} | all-to-all | bytes 1310720 | tf_op jit(solution)/shard_map/all_to_all | solution.py:54
  55.5 0.2 fusion.20
  55.6 0.1 copy.33
  55.7 0.1 copy.34
  55.9 0.1 exponential_bitcast_fusion
  55.9 0.2 fusion.16
  56.1 0.1 copy.24
  56.2 0.1 fusion.4
  56.3 0.1 copy.29
  56.5 0.0 copy-done
  56.5 0.0 copy-done.2
  56.5 0.5 fusion.3
  57.0 0.6 reshape.42
  57.6 0.3 constant_dynamic-slice_fusion.1
  57.9 0.1 copy.44
  58.0 4.8 %collective-permute-start.1 = (f32[32,8,112]{2,1,0:T(8,128)S(1)}, f32[32,8,112]{2,1,0:T(8,128)S(1)}, u32[]{:S(2)}, u32[]{:S(2)}) collective-permute-start(f32[32,8,112]{2,1,0:T(8,128)S(1)} %bitcast.49), channel_id=1, source_target_pairs={{0,1},{1,0},{2,3},{3,2},{4,5},{5,4},{6,7},{7,6},{8,9},{9,8},{10,11... | collective-permute-start | bytes 344072 | tf_op jit(solution)/shard_map/ppermute | solution.py:14
  62.8 1.0 %collective-permute-done.1 = f32[32,8,112]{2,1,0:T(8,128)S(1)} collective-permute-done((f32[32,8,112]{2,1,0:T(8,128)S(1)}, f32[32,8,112]{2,1,0:T(8,128)S(1)}, u32[]{:S(2)}, u32[]{:S(2)}) %collective-permute-start.1) | collective-permute-done | bytes 114720 | tf_op jit(solution)/shard_map/ppermute | solution.py:14
  63.8 0.1 fusion.11
  63.9 14.5 %all_to_all.11 = f32[32,8,112]{2,1,0:T(8,128)S(1)} all-to-all(f32[32,8,112]{2,1,0:T(8,128)S(1)} %fusion.11), channel_id=1, replica_groups={{0,2,4,6,8,10,12,14,16,18,20,22,24,26,28,30,32,34,36,38,40,42,44,46,48,..., dimensions={0} | all-to-all | bytes 229376 | tf_op jit(solution)/shard_map/all_to_all | solution.py:70
  78.4 0.6 reduce_sum.39
  (3 shorter events, 0.0 us)
Async XLA Ops:
  0.0 56.5 %copy-start = (bf16[128,7168]{1,0:T(8,128)(2,1)S(1)}, bf16[128,7168]{1,0:T(8,128)(2,1)}, u32[]{:S(2)}) copy-start(bf16[128,7168]{1,0:T(8,128)(2,1)} %param.9) | copy-start | bytes 5505028
  0.0 3.8 %copy-start.1 = (bf16[8,256,576]{1,2,0:T(8,128)(2,1)S(1)}, bf16[8,256,576]{1,2,0:T(8,128)(2,1)}, u32[]{:S(2)}) copy-start(bf16[8,256,576]{1,2,0:T(8,128)(2,1)} %param.6) | copy-start | bytes 7077892
  10.5 12.3 %collective-permute-start = (f32[32,8,640]{2,1,0:T(8,128)S(1)}, f32[32,8,640]{2,1,0:T(8,128)S(1)}, u32[]{:S(2)}, u32[]{:S(2)}) collective-permute-start(f32[32,8,640]{2,1,0:T(8,128)S(1)} %bitcast.48), channel_id=1, source_target_pairs={{0,1},{1,0},{2,3},{3,2},{4,5},{5,4},{6,7},{7,6},{8,9},{9,8},{10,11... | collective-permute-start | bytes 1966088 | tf_op jit(solution)/shard_map/ppermute | solution.py:14
  31.4 25.1 %copy-start.2 = (bf16[1,512,128]{2,1,0:T(8,128)(2,1)S(1)}, bf16[1,512,128]{2,1,0:T(8,128)(2,1)}, u32[]{:S(2)}) copy-start(bf16[1,512,128]{2,1,0:T(8,128)(2,1)} %param.8) | copy-start | bytes 393220
  58.0 5.8 %collective-permute-start.1 = (f32[32,8,112]{2,1,0:T(8,128)S(1)}, f32[32,8,112]{2,1,0:T(8,128)S(1)}, u32[]{:S(2)}, u32[]{:S(2)}) collective-permute-start(f32[32,8,112]{2,1,0:T(8,128)S(1)} %bitcast.49), channel_id=1, source_target_pairs={{0,1},{1,0},{2,3},{3,2},{4,5},{5,4},{6,7},{7,6},{8,9},{9,8},{10,11... | collective-permute-start | bytes 344072 | tf_op jit(solution)/shard_map/ppermute | solution.py:14

commit v2 on v0

v2 whole, which is shorter than its diff:
```python
import jax
import jax.numpy as jnp
from jax import lax
from jax.experimental import pallas as pl
from jax.experimental.pallas import tpu as pltpu
from jax.sharding import PartitionSpec as P

LATENT = 512
LANES = 128
TILES = LATENT // LANES
HALF = LANES // 2

softmax_scale = 192.0 ** (-0.5)
masked_value = -1e30


def vmem_specs(n):
    return [pl.BlockSpec(memory_space=pltpu.VMEM)] * n


def in_hbm(x):
    return pltpu.with_memory_space_constraint(x, pltpu.HBM)


def lane_of(rows):
    return lax.broadcasted_iota(jnp.int32, (rows, LANES), 1)


def attend(lengths, queries, cache, theirs, mine, l_buf, q_buf, k_buf, s_buf, arrived):
    rows, heads, _ = queries.shape
    shard_len = cache.shape[2]
    pairs = heads // 2
    block = rows * (TILES + 1)
    me = lax.axis_index("kv")
    first_core = lax.rem(me, 2) == 0
    small = [
        pltpu.make_async_copy(lengths, l_buf, arrived.at[rows]),
        pltpu.make_async_copy(queries, q_buf, arrived.at[rows + 1]),
    ]
    large = [pltpu.make_async_copy(cache.at[r], k_buf.at[r], arrived.at[r]) for r in range(rows)]
    for copy in small + large:
        copy.start()
    position = me * shard_len + lax.broadcasted_iota(jnp.int32, (1, shard_len), 1)
    first_half = lane_of(pairs) < HALF
    live, weights, stats = {}, {}, {}

    def score(r):
        live[r] = position < l_buf[r]
        scores = jnp.dot(q_buf[r], k_buf[r], preferred_element_type=jnp.float32) * softmax_scale
        scores = jnp.where(live[r], scores, masked_value)
        for t in range(shard_len // LANES):
            s_buf[r, t] = scores[:, t * LANES : (t + 1) * LANES]

    def soften(r):
        exponents, packed = [], []
        for parity in range(2):
            part = jnp.concatenate(
                [s_buf[r, t, pl.ds(parity, pairs, stride=2), :] for t in range(shard_len // LANES)],
                axis=1,
            )
            top = jnp.max(part, axis=1, keepdims=True)
            exponent = jnp.where(live[r], jnp.exp(part - top), 0.0)
            exponents.append(exponent)
            packed.append(jnp.where(first_half, top, jnp.sum(exponent, axis=1, keepdims=True)))
        even, odd = exponents
        weights[r] = jnp.concatenate(
            [jnp.where(first_core, odd, even), jnp.where(first_core, even, odd)], axis=0
        ).astype(jnp.bfloat16)
        even, odd = packed
        stats[r] = jnp.where(first_core, odd, even), jnp.where(first_core, even, odd)

    def weigh(r):
        numerators = lax.dot_general(
            weights[r],
            k_buf[r, :LATENT, :],
            (((1,), (1,)), ((), ())),
            preferred_element_type=jnp.float32,
        )
        for k, out in enumerate((theirs, mine)):
            part = numerators[k * pairs : (k + 1) * pairs]
            for t in range(TILES):
                out[pl.ds(t * rows + r, pairs, stride=block), :] = part[:, t * LANES : (t + 1) * LANES]
            out[pl.ds(TILES * rows + r, pairs, stride=block), :] = stats[r][k]

    for copy in small:
        copy.wait()
    groups = 2
    size = rows // groups
    for step in range(groups + 2):
        if step < groups:
            for r in range(step * size, (step + 1) * size):
                large[r].wait()
        for group, stage in ((step - 2, weigh), (step - 1, soften), (step, score)):
            if 0 <= group < groups:
                for r in range(group * size, (group + 1) * size):
                    stage(r)


def merge_cores(rows, got, mine, merged):
    block = rows * (TILES + 1)
    sent = rows * TILES + 1
    lane = lane_of(rows)
    first_half = lane < HALF
    diagonal = lax.rem(lane, HALF) == lax.broadcasted_iota(jnp.int32, (rows, LANES), 0)
    for q in range(got.shape[0] // block):
        stats = [ref[q * block + rows * TILES : (q + 1) * block, :] for ref in (got, mine)]
        tops = [jnp.where(first_half, s, pltpu.roll(s, HALF, 1)) for s in stats]
        top = jnp.maximum(*tops)
        weights = [jnp.exp(t - top) for t in tops]
        for t in range(TILES):
            at = pl.ds(q * block + t * rows, rows)
            merged[q * sent + t * rows : q * sent + (t + 1) * rows, :] = (
                got[at, :] * weights[0] + mine[at, :] * weights[1]
            )
        both = jnp.where(first_half, top, stats[0] * weights[0] + stats[1] * weights[1])
        merged[q * sent + TILES * rows : (q + 1) * sent, :] = jnp.sum(
            jnp.where(diagonal, both, 0.0), axis=0, keepdims=True
        )


def project(rows, got, value_up, out_proj, theirs, mine):
    sent = rows * TILES + 1
    chips = got.shape[0] // sent
    features = out_proj.shape[1] // (2 * chips)
    core = lax.rem(lax.axis_index("kv"), 2)
    stats = got[pl.ds(TILES * rows, chips, stride=sent), :]
    weight = jnp.exp(stats - jnp.max(stats, axis=0, keepdims=True))
    total = jnp.sum(weight * pltpu.roll(stats, HALF, 1), axis=0, keepdims=True)
    coefficient = jnp.transpose(jnp.where(lane_of(chips) < rows, weight / total, 0.0))[:rows]
    combined = [jnp.zeros((rows, LANES), jnp.float32) for _ in range(TILES)]
    for j in range(chips):
        factor = jnp.broadcast_to(coefficient[:, j : j + 1], (rows, LANES))
        for t in range(TILES):
            combined[t] += factor * got[j * sent + t * rows : j * sent + (t + 1) * rows, :]
    head_values = jnp.dot(
        jnp.concatenate(combined, axis=1).astype(jnp.bfloat16),
        value_up[0],
        preferred_element_type=jnp.float32,
    )
    projection = jnp.dot(
        head_values.astype(jnp.bfloat16), out_proj[...], preferred_element_type=jnp.float32
    )
    pad = jnp.zeros((rows, LANES - features), jnp.float32)
    for q in range(chips):
        blocks = [
            jnp.concatenate([projection[:, d * features : (d + 1) * features], pad], axis=1)
            for d in (2 * q, 2 * q + 1)
        ]
        theirs[q] = jnp.where(core == 0, blocks[1], blocks[0])
        mine[q] = jnp.where(core == 0, blocks[0], blocks[1])


def core_swap(x, kv):
    return lax.ppermute(x, "kv", [(i, i ^ 1) for i in range(kv)])


def on_device(kv, queries, latent_cache, lengths, value_up, out_proj):
    rows, heads, width = queries.shape
    shard_len = latent_cache.shape[1]
    chips = kv // 2
    same_core = [[2 * i + c for i in range(chips)] for c in range(2)]
    params = pltpu.CompilerParams(vmem_limit_bytes=40 * 2**20)
    f32 = jnp.float32

    block = rows * (TILES + 1)
    sent = rows * TILES + 1
    partials = jax.ShapeDtypeStruct((chips * block, LANES), f32)
    theirs, mine = pl.pallas_call(
        attend,
        out_shape=[partials] * 2,
        in_specs=[pl.BlockSpec(memory_space=pltpu.HBM)] * 3,
        out_specs=vmem_specs(2),
        scratch_shapes=[
            pltpu.SMEM((rows,), lengths.dtype),
            pltpu.VMEM((rows, heads, width), queries.dtype),
            pltpu.VMEM((rows, width, shard_len), latent_cache.dtype),
            pltpu.VMEM((rows, shard_len // LANES, heads, LANES), f32),
            pltpu.SemaphoreType.DMA((rows + 2,)),
        ],
        compiler_params=params,
    )(*[in_hbm(v) for v in (lengths, queries, latent_cache.transpose(0, 2, 1))])
    got = core_swap(theirs, kv)
    merged = pl.pallas_call(
        lambda *refs: merge_cores(rows, *refs),
        out_shape=jax.ShapeDtypeStruct((chips * sent, LANES), f32),
        in_specs=vmem_specs(2),
        out_specs=vmem_specs(1)[0],
        compiler_params=params,
    )(got, mine)
    got = lax.all_to_all(
        merged.reshape(chips, 1, sent * LANES), "kv", 0, 0, axis_index_groups=same_core
    ).reshape(chips * sent, LANES)
    features = jax.ShapeDtypeStruct((chips, rows, LANES), f32)
    theirs, mine = pl.pallas_call(
        lambda *refs: project(rows, *refs),
        out_shape=[features] * 2,
        in_specs=vmem_specs(3),
        out_specs=vmem_specs(2),
        compiler_params=params,
    )(got, value_up, out_proj)
    summed = mine + core_swap(theirs, kv)
    parts = lax.all_to_all(summed, "kv", 0, 0, axis_index_groups=same_core)
    return jnp.sum(parts, axis=0)[:, : out_proj.shape[1] // kv].astype(jnp.bfloat16)


def solution(mesh):
    kv = mesh.shape["kv"]
    placed = (
        P("rep", None, None),
        P("rep", "kv", None),
        P("rep"),
        P("kv", None, None),
        P("kv", None),
    )

    def device_step(*args):
        return on_device(kv, *args)

    return jax.shard_map(
        device_step, mesh=mesh, in_specs=placed, out_specs=P("rep", "kv"), check_vma=False
    )
```

time: 241 us -> 55.5 us (0.23); the launches traced: 237 us -> 54.7 us
  waiting for transfers between devices: 189 us -> 2.67 us
  blocking collectives: 0 us -> 33 us
  between operations: 13.5 us -> 0.04 us
  matrix products: 7.52 us -> 0 us
  starting transfers between devices: 21.4 us -> 14.3 us
  local copies, waits for them, and re-layouts: 4.44 us -> 0.01 us
  Pallas kernels: 0 us -> 4.13 us
    unnamed x2 -> x0, waiting for transfers between devices: 146 us -> none
    all_to_all x3 -> x0, waiting for transfers between devices: 42.4 us -> none  [the longest x1 28.4 us: on_device(): lax.all_to_all(partial_wide[None], 'kv', split_axis=2, concat_axis=0, til...]
    all_to_all x0 -> x2, blocking collectives: none -> 33 us  [the longest x1 18.5 us: on_device(): lax.all_to_all(merged.reshape(chips, 1, sent * LANES), 'kv', 0, 0, axis_i...]
    all_to_all x3 -> x0, starting transfers between devices: 21.3 us -> none  [the longest x1 11.6 us: on_device(): lax.all_to_all(totals[None], 'kv', split_axis=2, concat_axis=0, tiled=True)]
    ppermute x0 -> x2, starting transfers between devices: none -> 14.3 us  [core_swap(): return lax.ppermute(x, 'kv', [(i, i ^ 1) for i in range(kv)])]
    dot_general x2 -> x0, matrix products: 4.88 us -> none  [the longest x1 2.51 us: on_device(): jnp.einsum('rhk,rsk->rhs', queries, latent_cache, preferred_element_type=...]
    pallas_call x0 -> x3, Pallas kernels: none -> 4.13 us  [the longest x1 3.1 us: on_device(): pl.pallas_call(attend, out_shape=[partials] * 2, in_specs=[pl.BlockSpec(m...]
    broadcast_in_dim x3 -> x0, local copies, waits for them, and re-layouts: 2.97 us -> none  [the longest x1 1.6 us: on_device(): partial_wide[None]]
  transfers between devices with their start and end apart: 4 -> 2, of which waited for: 4 -> 2; matrix products, arithmetic and copies ran while one was open for 2% -> 0% of each run, Pallas kernels for 0% -> 0%
where the time goes in v2:
time: 55.5 us; the launch traced here: 54.7 us
  blocking collectives  33 us (59%)
  starting transfers between devices  14.3 us (26%)
  Pallas kernels  4.13 us (7%)
  waiting for transfers between devices  2.67 us (5%)
  other arithmetic  0.63 us (1%)
    all_to_all x1, blocking collectives, on_device(): lax.all_to_all(merged.reshape(chips, 1, sent * LANES), 'kv', 0, 0, axis_i...  18.5 us
    all_to_all x1, blocking collectives, on_device(): parts = lax.all_to_all(summed, 'kv', 0, 0, axis_index_groups=same_core)  14.5 us
    ppermute x2, starting transfers between devices, core_swap(): return lax.ppermute(x, 'kv', [(i, i ^ 1) for i in range(kv)])  14.3 us
    pallas_call x1, Pallas kernels, on_device(): pl.pallas_call(attend, out_shape=[partials] * 2, in_specs=[pl.BlockSpec(m...  3.1 us
    ppermute x2, waiting for transfers between devices, core_swap(): return lax.ppermute(x, 'kv', [(i, i ^ 1) for i in range(kv)])  2.67 us
  transfers between devices with their start and end apart: 2, of which 2 were waited for; matrix products, arithmetic and copies ran while one was open for 0% of the time, Pallas kernels for 0%

profile of v2, /device:TPU:1, one launch (start us, length us, event | category | flops | bytes accessed | tf_op | source)
XLA Modules:
  0.0 54.7 jit_solution(16345289084842164587)
XLA Ops:
  0.0 0.0 copy-start
  0.0 0.0 copy-start.1
  0.0 3.1 %shard_map.55 = (f32[1280,128]{1,0:T(8,128)S(1)}, f32[1280,128]{1,0:T(8,128)S(1)}) custom-call(s32[8]{0:T(128)} %lengths.1, bf16[8,64,576]{2,1,0:T(8,128)(2,1)} %queries.1, bf16[8,576,256]{2,1,0:T(8,128)(2,1)} %bitcast.6), custom_call_target="tpu_custom_call" | custom-call | tf_op jit(solution)/shard_map/pallas_call | solution.py:168
  3.1 8.8 %collective-permute-start = (f32[1280,128]{1,0:T(8,128)S(1)}, f32[1280,128]{1,0:T(8,128)S(1)}, u32[]{:S(2)}, u32[]{:S(2)}) collective-permute-start(f32[1280,128]{1,0:T(8,128)S(1)} %get-tuple-element.9), channel_id=1, source_target_pairs={{0,1},{1,0},{2,3},{3,2},{4,5},{5,4},{6,7},{7,6},{8,9},{9,8},{10,11... | collective-permute-start | bytes 1966088 | tf_op jit(solution)/shard_map/ppermute | solution.py:154
  11.9 1.7 %collective-permute-done.refs_0_ = f32[1280,128]{1,0:T(8,128)S(1)} collective-permute-done((f32[1280,128]{1,0:T(8,128)S(1)}, f32[1280,128]{1,0:T(8,128)S(1)}, u32[]{:S(2)}, u32[]{:S(2)}) %collective-permute-start) | collective-permute-done | bytes 655392 | tf_op jit(solution)/shard_map/ppermute | solution.py:154
  13.6 0.2 shard_map.56
  13.8 18.5 %all_to_all.10 = f32[32,1,4224]{2,1,0:T(1,128)S(1)} all-to-all(f32[32,1,4224]{2,1,0:T(1,128)S(1)} %bitcast.5), channel_id=1, replica_groups={{0,2,4,6,8,10,12,14,16,18,20,22,24,26,28,30,32,34,36,38,40,42,44,46,48,..., dimensions={0} | all-to-all | bytes 1081344 | tf_op jit(solution)/shard_map/all_to_all | solution.py:190
  32.4 0.0 copy-done
  32.4 0.0 copy-done.1
  32.4 0.8 %shard_map.57 = (f32[32,8,128]{2,1,0:T(8,128)S(1)}, f32[32,8,128]{2,1,0:T(8,128)S(1)}) custom-call(f32[1056,128]{1,0:T(8,128)S(1)} %bitcast.4, bf16[1,512,128]{2,1,0:T(8,128)(2,1)S(1)} %copy-done.1, bf16[128,7168]{1,0:T(8,128)(2,1)S(1)} %copy-done), custom_call_target="tpu_custom_call" | custom-call | tf_op jit(solution)/shard_map/pallas_call | solution.py:194
  33.2 5.5 %collective-permute-start.1 = (f32[32,8,128]{2,1,0:T(8,128)S(1)}, f32[32,8,128]{2,1,0:T(8,128)S(1)}, u32[]{:S(2)}, u32[]{:S(2)}) collective-permute-start(f32[32,8,128]{2,1,0:T(8,128)S(1)} %get-tuple-element.12), channel_id=1, source_target_pairs={{0,1},{1,0},{2,3},{3,2},{4,5},{5,4},{6,7},{7,6},{8,9},{9,8},{10,11... | collective-permute-start | bytes 393224 | tf_op jit(solution)/shard_map/ppermute | solution.py:154
  38.7 1.0 %collective-permute-done.1 = f32[32,8,128]{2,1,0:T(8,128)S(1)} collective-permute-done((f32[32,8,128]{2,1,0:T(8,128)S(1)}, f32[32,8,128]{2,1,0:T(8,128)S(1)}, u32[]{:S(2)}, u32[]{:S(2)}) %collective-permute-start.1) | collective-permute-done | bytes 131104 | tf_op jit(solution)/shard_map/ppermute | solution.py:154
  39.7 14.5 %all_to_all.11 = f32[32,8,128]{2,1,0:T(8,128)S(1)} all-to-all(f32[32,8,128]{2,1,0:T(8,128)S(1)} %add.3), channel_id=1, replica_groups={{0,2,4,6,8,10,12,14,16,18,20,22,24,26,28,30,32,34,36,38,40,42,44,46,48,..., dimensions={0} | all-to-all | bytes 262144 | tf_op jit(solution)/shard_map/all_to_all | solution.py:202
  54.1 0.6 %reduce_sum.9 = bf16[8,128]{1,0:T(8,128)(2,1)} reduce(f32[32,8,128]{2,1,0:T(8,128)S(1)} %all_to_all.11, f32[]{:T(128)} %constant.0.clone.1), dimensions={0}, to_apply=%region_0.0 | reduce | flops 31744 | bytes 133124 | tf_op jit(solution)/shard_map/reduce_sum | solution.py:203
  (1 shorter events, 0.0 us)
Async XLA Ops:
  0.0 32.4 %copy-start = (bf16[128,7168]{1,0:T(8,128)(2,1)S(1)}, bf16[128,7168]{1,0:T(8,128)(2,1)}, u32[]{:S(2)}) copy-start(bf16[128,7168]{1,0:T(8,128)(2,1)} %refs_2_.1) | copy-start | bytes 5505028
  0.0 32.4 %copy-start.1 = (bf16[1,512,128]{2,1,0:T(8,128)(2,1)S(1)}, bf16[1,512,128]{2,1,0:T(8,128)(2,1)}, u32[]{:S(2)}) copy-start(bf16[1,512,128]{2,1,0:T(8,128)(2,1)} %refs_1_.1) | copy-start | bytes 393220
  3.1 10.5 %collective-permute-start = (f32[1280,128]{1,0:T(8,128)S(1)}, f32[1280,128]{1,0:T(8,128)S(1)}, u32[]{:S(2)}, u32[]{:S(2)}) collective-permute-start(f32[1280,128]{1,0:T(8,128)S(1)} %get-tuple-element.9), channel_id=1, source_target_pairs={{0,1},{1,0},{2,3},{3,2},{4,5},{5,4},{6,7},{7,6},{8,9},{9,8},{10,11... | collective-permute-start | bytes 1966088 | tf_op jit(solution)/shard_map/ppermute | solution.py:154
  33.2 6.5 %collective-permute-start.1 = (f32[32,8,128]{2,1,0:T(8,128)S(1)}, f32[32,8,128]{2,1,0:T(8,128)S(1)}, u32[]{:S(2)}, u32[]{:S(2)}) collective-permute-start(f32[32,8,128]{2,1,0:T(8,128)S(1)} %get-tuple-element.12), channel_id=1, source_target_pairs={{0,1},{1,0},{2,3},{3,2},{4,5},{5,4},{6,7},{7,6},{8,9},{9,8},{10,11... | collective-permute-start | bytes 393224 | tf_op jit(solution)/shard_map/ppermute | solution.py:154

commit v3 on v2

--- a/solution.py
+++ b/solution.py
@@ -26,11 +26,38 @@
     return lax.broadcasted_iota(jnp.int32, (rows, LANES), 1)
 
 
-def attend(lengths, queries, cache, theirs, mine, l_buf, q_buf, k_buf, s_buf, arrived):
-    rows, heads, _ = queries.shape
+def soften(s_buf, r, parity):
+    pairs = s_buf.shape[2] // 2
+    part = jnp.concatenate(
+        [s_buf[r, t, pl.ds(parity, pairs, stride=2), :] for t in range(s_buf.shape[1])], axis=1
+    )
+    top = jnp.max(part, axis=1, keepdims=True)
+    exponent = jnp.where(part > 0.5 * masked_value, jnp.exp(part - top), 0.0)
+    packed = jnp.where(lane_of(pairs) < HALF, top, jnp.sum(exponent, axis=1, keepdims=True))
+    return exponent, packed
+
+
+def soften_one(s_buf, r, odd_wanted):
+    even, odd = soften(s_buf, r, 0), soften(s_buf, r, 1)
+    exponent, packed = [jnp.where(odd_wanted, b, a) for a, b in zip(even, odd)]
+    return exponent.astype(jnp.bfloat16), packed
+
+
+def weigh(out, weights, packed, k_buf, r):
+    rows = k_buf.shape[0]
+    pairs = weights.shape[0]
+    block = rows * (TILES + 1)
+    numerators = lax.dot_general(
+        weights, k_buf[r, :LATENT, :], (((1,), (1,)), ((), ())), preferred_element_type=jnp.float32
+    )
+    for t in range(TILES):
+        out[pl.ds(t * rows + r, pairs, stride=block), :] = numerators[:, t * LANES : (t + 1) * LANES]
+    out[pl.ds(TILES * rows + r, pairs, stride=block), :] = packed
+
+
+def attend_theirs(lengths, queries, cache, theirs, s_buf, k_buf, l_buf, q_buf, arrived):
+    rows = queries.shape[0]
     shard_len = cache.shape[2]
-    pairs = heads // 2
-    block = rows * (TILES + 1)
     me = lax.axis_index("kv")
     first_core = lax.rem(me, 2) == 0
     small = [
@@ -41,46 +68,19 @@
     for copy in small + large:
         copy.start()
     position = me * shard_len + lax.broadcasted_iota(jnp.int32, (1, shard_len), 1)
-    first_half = lane_of(pairs) < HALF
-    live, weights, stats = {}, {}, {}
+    softened = {}
 
     def score(r):
-        live[r] = position < l_buf[r]
         scores = jnp.dot(q_buf[r], k_buf[r], preferred_element_type=jnp.float32) * softmax_scale
-        scores = jnp.where(live[r], scores, masked_value)
+        scores = jnp.where(position < l_buf[r], scores, masked_value)
         for t in range(shard_len // LANES):
             s_buf[r, t] = scores[:, t * LANES : (t + 1) * LANES]
 
-    def soften(r):
-        exponents, packed = [], []
-        for parity in range(2):
-            part = jnp.concatenate(
-                [s_buf[r, t, pl.ds(parity, pairs, stride=2), :] for t in range(shard_len // LANES)],
-                axis=1,
-            )
-            top = jnp.max(part, axis=1, keepdims=True)
-            exponent = jnp.where(live[r], jnp.exp(part - top), 0.0)
-            exponents.append(exponent)
-            packed.append(jnp.where(first_half, top, jnp.sum(exponent, axis=1, keepdims=True)))
-        even, odd = exponents
-        weights[r] = jnp.concatenate(
-            [jnp.where(first_core, odd, even), jnp.where(first_core, even, odd)], axis=0
-        ).astype(jnp.bfloat16)
-        even, odd = packed
-        stats[r] = jnp.where(first_core, odd, even), jnp.where(first_core, even, odd)
-
-    def weigh(r):
-        numerators = lax.dot_general(
-            weights[r],
-            k_buf[r, :LATENT, :],
-            (((1,), (1,)), ((), ())),
-            preferred_element_type=jnp.float32,
-        )
-        for k, out in enumerate((theirs, mine)):
-            part = numerators[k * pairs : (k + 1) * pairs]
-            for t in range(TILES):
-                out[pl.ds(t * rows + r, pairs, stride=block), :] = part[:, t * LANES : (t + 1) * LANES]
-            out[pl.ds(TILES * rows + r, pairs, stride=block), :] = stats[r][k]
+    def weights_of(r):
+        softened[r] = soften_one(s_buf, r, first_core)
+
+    def finish(r):
+        weigh(theirs, *softened[r], k_buf, r)
 
     for copy in small:
         copy.wait()
@@ -90,10 +90,17 @@
         if step < groups:
             for r in range(step * size, (step + 1) * size):
                 large[r].wait()
-        for group, stage in ((step - 2, weigh), (step - 1, soften), (step, score)):
+        for group, stage in ((step - 2, finish), (step - 1, weights_of), (step, score)):
             if 0 <= group < groups:
                 for r in range(group * size, (group + 1) * size):
                     stage(r)
+
+
+def attend_mine(s_buf, k_buf, mine):
+    first_core = lax.rem(lax.axis_index("kv"), 2) == 0
+    softened = [soften_one(s_buf, r, jnp.logical_not(first_core)) for r in range(k_buf.shape[0])]
+    for r, pair in enumerate(softened):
+        weigh(mine, *pair, k_buf, r)
 
 
 def merge_cores(rows, got, mine, merged):
@@ -140,14 +147,35 @@
     projection = jnp.dot(
         head_values.astype(jnp.bfloat16), out_proj[...], preferred_element_type=jnp.float32
     )
-    pad = jnp.zeros((rows, LANES - features), jnp.float32)
+    spare = LANES - features
+    lane = lane_of(rows)
+    pad = jnp.zeros((rows, spare), jnp.float32)
     for q in range(chips):
-        blocks = [
-            jnp.concatenate([projection[:, d * features : (d + 1) * features], pad], axis=1)
-            for d in (2 * q, 2 * q + 1)
-        ]
-        theirs[q] = jnp.where(core == 0, blocks[1], blocks[0])
-        mine[q] = jnp.where(core == 0, blocks[0], blocks[1])
+        blocks = []
+        for d in (2 * q, 2 * q + 1):
+            part = jnp.concatenate([projection[:, d * features : (d + 1) * features], pad], axis=1)
+            last = jnp.broadcast_to(part[rows - 1 :], (rows, LANES))
+            last = pltpu.roll(last, spare, 1, stride=spare, stride_axis=0)
+            blocks.append(jnp.where(lane < features, part, last))
+        at = pl.ds(q * (rows - 1), rows - 1)
+        theirs[at, :] = jnp.where(core == 0, blocks[1], blocks[0])[: rows - 1]
+        mine[at, :] = jnp.where(core == 0, blocks[0], blocks[1])[: rows - 1]
+
+
+def add_other(both, mine, out):
+    out[...] = mine[...] + both[1 - lax.rem(lax.axis_index("kv"), 2)]
+
+
+def add_up(got, out):
+    rows, features = out.shape
+    spare = LANES - features
+    total = got[pl.ds(0, rows - 1), :]
+    for j in range(1, got.shape[0] // (rows - 1)):
+        total += got[pl.ds(j * (rows - 1), rows - 1), :]
+    last = [total[i : i + 1, features:] for i in reversed(range(rows - 1))]
+    out[...] = jnp.concatenate(
+        [total[:, :features], jnp.concatenate(last, axis=1)], axis=0
+    ).astype(out.dtype)
 
 
 def core_swap(x, kv):
@@ -159,27 +187,36 @@
     shard_len = latent_cache.shape[1]
     chips = kv // 2
     same_core = [[2 * i + c for i in range(chips)] for c in range(2)]
-    params = pltpu.CompilerParams(vmem_limit_bytes=40 * 2**20)
+    params = pltpu.CompilerParams(vmem_limit_bytes=8 * 2**20)
     f32 = jnp.float32
 
     block = rows * (TILES + 1)
     sent = rows * TILES + 1
     partials = jax.ShapeDtypeStruct((chips * block, LANES), f32)
-    theirs, mine = pl.pallas_call(
-        attend,
-        out_shape=[partials] * 2,
+    theirs, scores, held = pl.pallas_call(
+        attend_theirs,
+        out_shape=[
+            partials,
+            jax.ShapeDtypeStruct((rows, shard_len // LANES, heads, LANES), f32),
+            jax.ShapeDtypeStruct((rows, width, shard_len), latent_cache.dtype),
+        ],
         in_specs=[pl.BlockSpec(memory_space=pltpu.HBM)] * 3,
-        out_specs=vmem_specs(2),
+        out_specs=vmem_specs(3),
         scratch_shapes=[
             pltpu.SMEM((rows,), lengths.dtype),
             pltpu.VMEM((rows, heads, width), queries.dtype),
-            pltpu.VMEM((rows, width, shard_len), latent_cache.dtype),
-            pltpu.VMEM((rows, shard_len // LANES, heads, LANES), f32),
             pltpu.SemaphoreType.DMA((rows + 2,)),
         ],
         compiler_params=params,
     )(*[in_hbm(v) for v in (lengths, queries, latent_cache.transpose(0, 2, 1))])
     got = core_swap(theirs, kv)
+    mine = pl.pallas_call(
+        attend_mine,
+        out_shape=partials,
+        in_specs=vmem_specs(2),
+        out_specs=vmem_specs(1)[0],
+        compiler_params=params,
+    )(scores, held)
     merged = pl.pallas_call(
         lambda *refs: merge_cores(rows, *refs),
         out_shape=jax.ShapeDtypeStruct((chips * sent, LANES), f32),
@@ -190,7 +227,7 @@
     got = lax.all_to_all(
         merged.reshape(chips, 1, sent * LANES), "kv", 0, 0, axis_index_groups=same_core
     ).reshape(chips * sent, LANES)
-    features = jax.ShapeDtypeStruct((chips, rows, LANES), f32)
+    features = jax.ShapeDtypeStruct((chips * (rows - 1), LANES), f32)
     theirs, mine = pl.pallas_call(
         lambda *refs: project(rows, *refs),
         out_shape=[features] * 2,
@@ -198,9 +235,25 @@
         out_specs=vmem_specs(2),
         compiler_params=params,
     )(got, value_up, out_proj)
-    summed = mine + core_swap(theirs, kv)
-    parts = lax.all_to_all(summed, "kv", 0, 0, axis_index_groups=same_core)
-    return jnp.sum(parts, axis=0)[:, : out_proj.shape[1] // kv].astype(jnp.bfloat16)
+    both = lax.all_gather(
+        theirs, "kv", axis_index_groups=[[2 * i, 2 * i + 1] for i in range(chips)]
+    )
+    summed = pl.pallas_call(
+        add_other,
+        out_shape=features,
+        in_specs=vmem_specs(2),
+        out_specs=vmem_specs(1)[0],
+        compiler_params=params,
+    )(both, mine)
+    parts = lax.all_to_all(
+        summed.reshape(chips, 1, (rows - 1) * LANES), "kv", 0, 0, axis_index_groups=same_core
+    ).reshape(chips * (rows - 1), LANES)
+    return pl.pallas_call(
+        add_up,
+        out_shape=jax.ShapeDtypeStruct((rows, out_proj.shape[1] // kv), jnp.bfloat16),
+        in_specs=vmem_specs(1),
+        compiler_params=params,
+    )(parts)
 
 
 def solution(mesh):

time: 55.5 us -> 53.9 us (0.971)
  starting transfers between devices: 14.3 us -> 8.79 us
  blocking collectives: 33 us -> 38.1 us
  waiting for transfers between devices: 2.67 us -> 0.9 us
  Pallas kernels: 4.13 us -> 5.46 us
  other arithmetic: 0.63 us -> 0 us
    ppermute x2 -> x1, starting transfers between devices: 14.3 us -> 8.79 us  [core_swap(): return lax.ppermute(x, 'kv', [(i, i ^ 1) for i in range(kv)])]
    all_gather x0 -> x1, blocking collectives: none -> 5.19 us  [on_device(): lax.all_gather(theirs, 'kv', axis_index_groups=[[2 * i, 2 * i + 1] for i...]
    ppermute x2 -> x1, waiting for transfers between devices: 2.67 us -> 0.9 us  [core_swap(): return lax.ppermute(x, 'kv', [(i, i ^ 1) for i in range(kv)])]
    pallas_call x1 -> x4, Pallas kernels: 3.1 us -> 4.35 us  [the longest x1 2.87 us: on_device(): pl.pallas_call(attend_theirs, out_shape=[partials, jax.ShapeDtypeStruct((...]
    reduce_sum x1 -> x0, other arithmetic: 0.61 us -> none  [on_device(): jnp.sum(parts, axis=0)[:, :out_proj.shape[1] // kv].astype(jnp.bfloat16)]
  transfers between devices with their start and end apart: 2 -> 1, of which waited for: 2 -> 1; matrix products, arithmetic and copies ran while one was open for 0% -> 0% of each run, Pallas kernels for 0% -> 1%
where the time goes in v3:
time: 53.9 us; the launch traced here: 53.3 us
  blocking collectives  38.1 us (71%)
  starting transfers between devices  8.79 us (16%)
  Pallas kernels  5.46 us (10%)
  waiting for transfers between devices  0.9 us (2%)
    all_to_all x1, blocking collectives, on_device(): lax.all_to_all(merged.reshape(chips, 1, sent * LANES), 'kv', 0, 0, axis_i...  18.5 us
    all_to_all x1, blocking collectives, on_device(): lax.all_to_all(summed.reshape(chips, 1, (rows - 1) * LANES), 'kv', 0, 0,...  14.4 us
    ppermute x1, starting transfers between devices, core_swap(): return lax.ppermute(x, 'kv', [(i, i ^ 1) for i in range(kv)])  8.79 us
    all_gather x1, blocking collectives, on_device(): lax.all_gather(theirs, 'kv', axis_index_groups=[[2 * i, 2 * i + 1] for i...  5.19 us
    pallas_call x1, Pallas kernels, on_device(): pl.pallas_call(attend_theirs, out_shape=[partials, jax.ShapeDtypeStruct((...  2.87 us
  transfers between devices with their start and end apart: 1, of which 1 were waited for; matrix products, arithmetic and copies ran while one was open for 0% of the time, Pallas kernels for 1%

profile of v3, /device:TPU:1, one launch (start us, length us, event | category | flops | bytes accessed | tf_op | source)
XLA Modules:
  0.0 53.3 jit_solution(1517116122387334051)
XLA Ops:
  0.0 2.9 %shard_map.55 = (f32[1280,128]{1,0:T(8,128)S(1)}, f32[8,2,64,128]{3,2,1,0:T(8,128)S(1)}, bf16[8,576,256]{2,1,0:T(8,128)(2,1)S(1)}) custom-call(s32[8]{0:T(128)} %lengths.1, bf16[8,64,576]{2,1,0:T(8,128)(2,1)} %queries.1, bf16[8,576,256]{2,1,0:T(8,128)(2,1)} %bitcast.11), custom_call_target="tpu_custom_call" | custom-call | tf_op jit(solution)/shard_map/pallas_call | solution.py:196
  2.9 8.8 %collective-permute-start = (f32[1280,128]{1,0:T(8,128)S(1)}, f32[1280,128]{1,0:T(8,128)S(1)}, u32[]{:S(2)}, u32[]{:S(2)}) collective-permute-start(f32[1280,128]{1,0:T(8,128)S(1)} %get-tuple-element.10), channel_id=1, source_target_pairs={{0,1},{1,0},{2,3},{3,2},{4,5},{5,4},{6,7},{7,6},{8,9},{9,8},{10,11... | collective-permute-start | bytes 1966088 | tf_op jit(solution)/shard_map/ppermute | solution.py:182
  11.7 0.0 copy-start
  11.7 0.0 copy-start.1
  11.7 0.8 %shard_map.56.refs_1_ = f32[1280,128]{1,0:T(8,128)S(1)} custom-call(f32[8,2,64,128]{3,2,1,0:T(8,128)S(1)} %get-tuple-element.11.s_buf, bf16[8,576,256]{2,1,0:T(8,128)(2,1)S(1)} %get-tuple-element.12.k_buf), custom_call_target="tpu_custom_call" | custom-call | tf_op jit(solution)/shard_map/pallas_call | solution.py:213
  12.5 0.9 %collective-permute-done.refs_0_ = f32[1280,128]{1,0:T(8,128)S(1)} collective-permute-done((f32[1280,128]{1,0:T(8,128)S(1)}, f32[1280,128]{1,0:T(8,128)S(1)}, u32[]{:S(2)}, u32[]{:S(2)}) %collective-permute-start) | collective-permute-done | bytes 655392 | tf_op jit(solution)/shard_map/ppermute | solution.py:182
  13.4 0.2 shard_map.57
  13.6 18.5 %all_to_all.10 = f32[32,1,4224]{2,1,0:T(1,128)S(1)} all-to-all(f32[32,1,4224]{2,1,0:T(1,128)S(1)} %bitcast.7), channel_id=1, replica_groups={{0,2,4,6,8,10,12,14,16,18,20,22,24,26,28,30,32,34,36,38,40,42,44,46,48,..., dimensions={0} | all-to-all | bytes 1081344 | tf_op jit(solution)/shard_map/all_to_all | solution.py:227
  32.1 0.0 copy-done
  32.1 0.0 copy-done.1
  32.1 0.9 %shard_map.58 = (f32[224,128]{1,0:T(8,128)S(1)}, f32[224,128]{1,0:T(8,128)S(1)}) custom-call(f32[1056,128]{1,0:T(8,128)S(1)} %bitcast.6, bf16[1,512,128]{2,1,0:T(8,128)(2,1)S(1)} %copy-done.1, bf16[128,7168]{1,0:T(8,128)(2,1)S(1)} %copy-done), custom_call_target="tpu_custom_call" | custom-call | tf_op jit(solution)/shard_map/pallas_call | solution.py:231
  33.0 5.2 %all-gather = f32[448,128]{1,0:T(8,128)S(1)} all-gather(f32[224,128]{1,0:T(8,128)S(1)} %get-tuple-element.13), channel_id=2, replica_groups={{0,1},{2,3},{4,5},{6,7},{8,9},{10,11},{12,13},{14,15},{16,17},{18,19},{..., dimensions={0}, use_global_device_ids=true | all-gather | bytes 344064 | tf_op jit(solution)/shard_map/all_gather | solution.py:238
  38.2 14.4 %all_to_all.11 = f32[32,1,896]{2,1,0:T(1,128)S(1)} all-to-all(f32[32,1,896]{2,1,0:T(1,128)S(1)} %bitcast.9), channel_id=1, replica_groups={{0,2,4,6,8,10,12,14,16,18,20,22,24,26,28,30,32,34,36,38,40,42,44,46,48,..., dimensions={0} | all-to-all | bytes 229376 | tf_op jit(solution)/shard_map/all_to_all | solution.py:248
  52.6 0.7 %shard_map.60 = bf16[8,112]{1,0:T(8,128)(2,1)} custom-call(f32[224,128]{1,0:T(8,128)S(1)} %bitcast.10), custom_call_target="tpu_custom_call" | custom-call | tf_op jit(solution)/shard_map/pallas_call | solution.py:251
  (1 shorter events, 0.0 us)
Async XLA Ops:
  2.9 10.5 %collective-permute-start = (f32[1280,128]{1,0:T(8,128)S(1)}, f32[1280,128]{1,0:T(8,128)S(1)}, u32[]{:S(2)}, u32[]{:S(2)}) collective-permute-start(f32[1280,128]{1,0:T(8,128)S(1)} %get-tuple-element.10), channel_id=1, source_target_pairs={{0,1},{1,0},{2,3},{3,2},{4,5},{5,4},{6,7},{7,6},{8,9},{9,8},{10,11... | collective-permute-start | bytes 1966088 | tf_op jit(solution)/shard_map/ppermute | solution.py:182
  11.7 20.5 %copy-start = (bf16[128,7168]{1,0:T(8,128)(2,1)S(1)}, bf16[128,7168]{1,0:T(8,128)(2,1)}, u32[]{:S(2)}) copy-start(bf16[128,7168]{1,0:T(8,128)(2,1)} %refs_2_.1) | copy-start | bytes 5505028
  11.7 20.4 %copy-start.1 = (bf16[1,512,128]{2,1,0:T(8,128)(2,1)S(1)}, bf16[1,512,128]{2,1,0:T(8,128)(2,1)}, u32[]{:S(2)}) copy-start(bf16[1,512,128]{2,1,0:T(8,128)(2,1)} %refs_1_.1) | copy-start | bytes 393220

commit v4 on v3

--- a/solution.py
+++ b/solution.py
@@ -84,16 +84,11 @@
 
     for copy in small:
         copy.wait()
-    groups = 2
-    size = rows // groups
-    for step in range(groups + 2):
-        if step < groups:
-            for r in range(step * size, (step + 1) * size):
-                large[r].wait()
-        for group, stage in ((step - 2, finish), (step - 1, weights_of), (step, score)):
-            if 0 <= group < groups:
-                for r in range(group * size, (group + 1) * size):
-                    stage(r)
+    for copy in large:
+        copy.wait()
+    for stage in (score, weights_of, finish):
+        for r in range(rows):
+            stage(r)
 
 
 def attend_mine(s_buf, k_buf, mine):
@@ -103,29 +98,29 @@
         weigh(mine, *pair, k_buf, r)
 
 
-def merge_cores(rows, got, mine, merged):
+def merge_cores(rows, order, got, mine, merged):
     block = rows * (TILES + 1)
     sent = rows * TILES + 1
     lane = lane_of(rows)
     first_half = lane < HALF
     diagonal = lax.rem(lane, HALF) == lax.broadcasted_iota(jnp.int32, (rows, LANES), 0)
-    for q in range(got.shape[0] // block):
+    for slot, q in enumerate(order):
         stats = [ref[q * block + rows * TILES : (q + 1) * block, :] for ref in (got, mine)]
         tops = [jnp.where(first_half, s, pltpu.roll(s, HALF, 1)) for s in stats]
         top = jnp.maximum(*tops)
         weights = [jnp.exp(t - top) for t in tops]
         for t in range(TILES):
             at = pl.ds(q * block + t * rows, rows)
-            merged[q * sent + t * rows : q * sent + (t + 1) * rows, :] = (
+            merged[slot * sent + t * rows : slot * sent + (t + 1) * rows, :] = (
                 got[at, :] * weights[0] + mine[at, :] * weights[1]
             )
         both = jnp.where(first_half, top, stats[0] * weights[0] + stats[1] * weights[1])
-        merged[q * sent + TILES * rows : (q + 1) * sent, :] = jnp.sum(
+        merged[slot * sent + TILES * rows : (slot + 1) * sent, :] = jnp.sum(
             jnp.where(diagonal, both, 0.0), axis=0, keepdims=True
         )
 
 
-def project(rows, got, value_up, out_proj, theirs, mine):
+def project(rows, order, got, value_up, out_proj, theirs, mine):
     sent = rows * TILES + 1
     chips = got.shape[0] // sent
     features = out_proj.shape[1] // (2 * chips)
@@ -150,14 +145,14 @@
     spare = LANES - features
     lane = lane_of(rows)
     pad = jnp.zeros((rows, spare), jnp.float32)
-    for q in range(chips):
+    for slot, q in enumerate(order):
         blocks = []
         for d in (2 * q, 2 * q + 1):
             part = jnp.concatenate([projection[:, d * features : (d + 1) * features], pad], axis=1)
             last = jnp.broadcast_to(part[rows - 1 :], (rows, LANES))
             last = pltpu.roll(last, spare, 1, stride=spare, stride_axis=0)
             blocks.append(jnp.where(lane < features, part, last))
-        at = pl.ds(q * (rows - 1), rows - 1)
+        at = pl.ds(slot * (rows - 1), rows - 1)
         theirs[at, :] = jnp.where(core == 0, blocks[1], blocks[0])[: rows - 1]
         mine[at, :] = jnp.where(core == 0, blocks[0], blocks[1])[: rows - 1]
 
@@ -182,11 +177,17 @@
     return lax.ppermute(x, "kv", [(i, i ^ 1) for i in range(kv)])
 
 
+def chip_order(chips):
+    first = 19 % chips
+    return [(first + i) % chips for i in range(chips)]
+
+
 def on_device(kv, queries, latent_cache, lengths, value_up, out_proj):
     rows, heads, width = queries.shape
     shard_len = latent_cache.shape[1]
     chips = kv // 2
-    same_core = [[2 * i + c for i in range(chips)] for c in range(2)]
+    order = chip_order(chips)
+    same_core = [[2 * i + c for i in order] for c in range(2)]
     params = pltpu.CompilerParams(vmem_limit_bytes=8 * 2**20)
     f32 = jnp.float32
 
@@ -218,7 +219,7 @@
         compiler_params=params,
     )(scores, held)
     merged = pl.pallas_call(
-        lambda *refs: merge_cores(rows, *refs),
+        lambda *refs: merge_cores(rows, order, *refs),
         out_shape=jax.ShapeDtypeStruct((chips * sent, LANES), f32),
         in_specs=vmem_specs(2),
         out_specs=vmem_specs(1)[0],
@@ -229,7 +230,7 @@
     ).reshape(chips * sent, LANES)
     features = jax.ShapeDtypeStruct((chips * (rows - 1), LANES), f32)
     theirs, mine = pl.pallas_call(
-        lambda *refs: project(rows, *refs),
+        lambda *refs: project(rows, order, *refs),
         out_shape=[features] * 2,
         in_specs=vmem_specs(3),
         out_specs=vmem_specs(2),

time: 53.9 us -> 51.9 us (0.963)
  blocking collectives: 38.1 us -> 36.2 us
    all_to_all x1, blocking collectives: 14.4 us -> 12 us  [on_device(): lax.all_to_all(summed.reshape(chips, 1, (rows - 1) * LANES), 'kv', 0, 0,...]
    all_to_all x1, blocking collectives: 18.5 us -> 20.8 us  [on_device(): lax.all_to_all(merged.reshape(chips, 1, sent * LANES), 'kv', 0, 0, axis_i...]
    all_gather x1, blocking collectives: 5.19 us -> 3.42 us  [on_device(): lax.all_gather(theirs, 'kv', axis_index_groups=[[2 * i, 2 * i + 1] for i...]
  transfers between devices with their start and end apart: 1 -> 1, of which waited for: 1 -> 1; matrix products, arithmetic and copies ran while one was open for 0% -> 0% of each run, Pallas kernels for 1% -> 2%
where the time goes in v4:
time: 51.9 us; the launch traced here: 51.6 us
  blocking collectives  36.2 us (70%)
  starting transfers between devices  8.8 us (17%)
  Pallas kernels  5.67 us (11%)
  waiting for transfers between devices  0.9 us (2%)
    all_to_all x1, blocking collectives, on_device(): lax.all_to_all(merged.reshape(chips, 1, sent * LANES), 'kv', 0, 0, axis_i...  20.8 us
    all_to_all x1, blocking collectives, on_device(): lax.all_to_all(summed.reshape(chips, 1, (rows - 1) * LANES), 'kv', 0, 0,...  12 us
    ppermute x1, starting transfers between devices, core_swap(): return lax.ppermute(x, 'kv', [(i, i ^ 1) for i in range(kv)])  8.8 us
    all_gather x1, blocking collectives, on_device(): lax.all_gather(theirs, 'kv', axis_index_groups=[[2 * i, 2 * i + 1] for i...  3.42 us
    pallas_call x1, Pallas kernels, on_device(): pl.pallas_call(attend_theirs, out_shape=[partials, jax.ShapeDtypeStruct((...  3.08 us
  transfers between devices with their start and end apart: 1, of which 1 were waited for; matrix products, arithmetic and copies ran while one was open for 0% of the time, Pallas kernels for 2%

profile of v4, /device:TPU:1, one launch (start us, length us, event | category | flops | bytes accessed | tf_op | source)
XLA Modules:
  0.0 51.6 jit_solution(12151091463457206006)
XLA Ops:
  0.0 3.1 %shard_map.55 = (f32[1280,128]{1,0:T(8,128)S(1)}, f32[8,2,64,128]{3,2,1,0:T(8,128)S(1)}, bf16[8,576,256]{2,1,0:T(8,128)(2,1)S(1)}) custom-call(s32[8]{0:T(128)} %lengths.1, bf16[8,64,576]{2,1,0:T(8,128)(2,1)} %queries.1, bf16[8,576,256]{2,1,0:T(8,128)(2,1)} %bitcast.11), custom_call_target="tpu_custom_call" | custom-call | tf_op jit(solution)/shard_map/pallas_call | solution.py:197
  3.1 8.8 %collective-permute-start = (f32[1280,128]{1,0:T(8,128)S(1)}, f32[1280,128]{1,0:T(8,128)S(1)}, u32[]{:S(2)}, u32[]{:S(2)}) collective-permute-start(f32[1280,128]{1,0:T(8,128)S(1)} %get-tuple-element.10), channel_id=1, source_target_pairs={{0,1},{1,0},{2,3},{3,2},{4,5},{5,4},{6,7},{7,6},{8,9},{9,8},{10,11... | collective-permute-start | bytes 1966088 | tf_op jit(solution)/shard_map/ppermute | solution.py:177
  11.9 0.0 copy-start
  11.9 0.0 copy-start.1
  11.9 0.8 %shard_map.56.refs_1_ = f32[1280,128]{1,0:T(8,128)S(1)} custom-call(f32[8,2,64,128]{3,2,1,0:T(8,128)S(1)} %get-tuple-element.11.s_buf, bf16[8,576,256]{2,1,0:T(8,128)(2,1)S(1)} %get-tuple-element.12.k_buf), custom_call_target="tpu_custom_call" | custom-call | tf_op jit(solution)/shard_map/pallas_call | solution.py:214
  12.7 0.9 %collective-permute-done.refs_0_ = f32[1280,128]{1,0:T(8,128)S(1)} collective-permute-done((f32[1280,128]{1,0:T(8,128)S(1)}, f32[1280,128]{1,0:T(8,128)S(1)}, u32[]{:S(2)}, u32[]{:S(2)}) %collective-permute-start) | collective-permute-done | bytes 655392 | tf_op jit(solution)/shard_map/ppermute | solution.py:177
  13.6 0.2 shard_map.57
  13.8 20.8 %all_to_all.10 = f32[32,1,4224]{2,1,0:T(1,128)S(1)} all-to-all(f32[32,1,4224]{2,1,0:T(1,128)S(1)} %bitcast.7), channel_id=1, replica_groups={{38,40,42,44,46,48,50,52,54,56,58,60,62,0,2,4,6,8,10,12,14,16,18,20,22,..., dimensions={0} | all-to-all | bytes 1081344 | tf_op jit(solution)/shard_map/all_to_all | solution.py:228
  34.6 0.0 copy-done
  34.6 0.0 copy-done.1
  34.6 0.9 %shard_map.58 = (f32[224,128]{1,0:T(8,128)S(1)}, f32[224,128]{1,0:T(8,128)S(1)}) custom-call(f32[1056,128]{1,0:T(8,128)S(1)} %bitcast.6, bf16[1,512,128]{2,1,0:T(8,128)(2,1)S(1)} %copy-done.1, bf16[128,7168]{1,0:T(8,128)(2,1)S(1)} %copy-done), custom_call_target="tpu_custom_call" | custom-call | tf_op jit(solution)/shard_map/pallas_call | solution.py:232
  35.5 3.4 %all-gather = f32[448,128]{1,0:T(8,128)S(1)} all-gather(f32[224,128]{1,0:T(8,128)S(1)} %get-tuple-element.13), channel_id=2, replica_groups={{0,1},{2,3},{4,5},{6,7},{8,9},{10,11},{12,13},{14,15},{16,17},{18,19},{..., dimensions={0}, use_global_device_ids=true | all-gather | bytes 344064 | tf_op jit(solution)/shard_map/all_gather | solution.py:239
  39.0 12.0 %all_to_all.11 = f32[32,1,896]{2,1,0:T(1,128)S(1)} all-to-all(f32[32,1,896]{2,1,0:T(1,128)S(1)} %bitcast.9), channel_id=1, replica_groups={{38,40,42,44,46,48,50,52,54,56,58,60,62,0,2,4,6,8,10,12,14,16,18,20,22,..., dimensions={0} | all-to-all | bytes 229376 | tf_op jit(solution)/shard_map/all_to_all | solution.py:249
  51.0 0.7 %shard_map.60 = bf16[8,112]{1,0:T(8,128)(2,1)} custom-call(f32[224,128]{1,0:T(8,128)S(1)} %bitcast.10), custom_call_target="tpu_custom_call" | custom-call | tf_op jit(solution)/shard_map/pallas_call | solution.py:252
  (1 shorter events, 0.0 us)
Async XLA Ops:
  3.1 10.5 %collective-permute-start = (f32[1280,128]{1,0:T(8,128)S(1)}, f32[1280,128]{1,0:T(8,128)S(1)}, u32[]{:S(2)}, u32[]{:S(2)}) collective-permute-start(f32[1280,128]{1,0:T(8,128)S(1)} %get-tuple-element.10), channel_id=1, source_target_pairs={{0,1},{1,0},{2,3},{3,2},{4,5},{5,4},{6,7},{7,6},{8,9},{9,8},{10,11... | collective-permute-start | bytes 1966088 | tf_op jit(solution)/shard_map/ppermute | solution.py:177
  11.9 22.7 %copy-start = (bf16[128,7168]{1,0:T(8,128)(2,1)S(1)}, bf16[128,7168]{1,0:T(8,128)(2,1)}, u32[]{:S(2)}) copy-start(bf16[128,7168]{1,0:T(8,128)(2,1)} %refs_2_.1) | copy-start | bytes 5505028
  11.9 22.7 %copy-start.1 = (bf16[1,512,128]{2,1,0:T(8,128)(2,1)S(1)}, bf16[1,512,128]{2,1,0:T(8,128)(2,1)}, u32[]{:S(2)}) copy-start(bf16[1,512,128]{2,1,0:T(8,128)(2,1)} %refs_1_.1) | copy-start | bytes 393220

commit v5 on v4

--- a/solution.py
+++ b/solution.py
@@ -26,37 +26,50 @@
     return lax.broadcasted_iota(jnp.int32, (rows, LANES), 1)
 
 
-def soften(s_buf, r, parity):
+def soften(s_buf, r, odd_wanted, stats):
     pairs = s_buf.shape[2] // 2
-    part = jnp.concatenate(
-        [s_buf[r, t, pl.ds(parity, pairs, stride=2), :] for t in range(s_buf.shape[1])], axis=1
-    )
+    even, odd = [
+        jnp.concatenate(
+            [s_buf[r, t, pl.ds(parity, pairs, stride=2), :] for t in range(s_buf.shape[1])], axis=1
+        )
+        for parity in range(2)
+    ]
+    part = jnp.where(odd_wanted, odd, even)
     top = jnp.max(part, axis=1, keepdims=True)
     exponent = jnp.where(part > 0.5 * masked_value, jnp.exp(part - top), 0.0)
-    packed = jnp.where(lane_of(pairs) < HALF, top, jnp.sum(exponent, axis=1, keepdims=True))
-    return exponent, packed
-
-
-def soften_one(s_buf, r, odd_wanted):
-    even, odd = soften(s_buf, r, 0), soften(s_buf, r, 1)
-    exponent, packed = [jnp.where(odd_wanted, b, a) for a, b in zip(even, odd)]
-    return exponent.astype(jnp.bfloat16), packed
-
-
-def weigh(out, weights, packed, k_buf, r):
+    lane = lane_of(pairs)
+    stats = jnp.where(lane == r, top, stats)
+    stats = jnp.where(lane == HALF + r, jnp.sum(exponent, axis=1, keepdims=True), stats)
+    return exponent.astype(jnp.bfloat16), stats
+
+
+def weigh(out, weights, k_buf, r):
     rows = k_buf.shape[0]
     pairs = weights.shape[0]
-    block = rows * (TILES + 1)
     numerators = lax.dot_general(
         weights, k_buf[r, :LATENT, :], (((1,), (1,)), ((), ())), preferred_element_type=jnp.float32
     )
     for t in range(TILES):
-        out[pl.ds(t * rows + r, pairs, stride=block), :] = numerators[:, t * LANES : (t + 1) * LANES]
-    out[pl.ds(TILES * rows + r, pairs, stride=block), :] = packed
+        out[pl.ds(t * rows + r, pairs, stride=rows * TILES + 1), :] = numerators[
+            :, t * LANES : (t + 1) * LANES
+        ]
+
+
+def finish(out, s_buf, k_buf, odd_wanted):
+    rows = k_buf.shape[0]
+    pairs = s_buf.shape[2] // 2
+    stats = jnp.zeros((pairs, LANES), jnp.float32)
+    weights = []
+    for r in range(rows):
+        exponent, stats = soften(s_buf, r, odd_wanted, stats)
+        weights.append(exponent)
+    for r in range(rows):
+        weigh(out, weights[r], k_buf, r)
+    out[pl.ds(rows * TILES, pairs, stride=rows * TILES + 1), :] = stats
 
 
 def attend_theirs(lengths, queries, cache, theirs, s_buf, k_buf, l_buf, q_buf, arrived):
-    rows = queries.shape[0]
+    rows, heads, _ = queries.shape
     shard_len = cache.shape[2]
     me = lax.axis_index("kv")
     first_core = lax.rem(me, 2) == 0
@@ -68,7 +81,8 @@
     for copy in small + large:
         copy.start()
     position = me * shard_len + lax.broadcasted_iota(jnp.int32, (1, shard_len), 1)
-    softened = {}
+    stats = [jnp.zeros((heads // 2, LANES), jnp.float32)]
+    weights = {}
 
     def score(r):
         scores = jnp.dot(q_buf[r], k_buf[r], preferred_element_type=jnp.float32) * softmax_scale
@@ -76,48 +90,47 @@
         for t in range(shard_len // LANES):
             s_buf[r, t] = scores[:, t * LANES : (t + 1) * LANES]
 
-    def weights_of(r):
-        softened[r] = soften_one(s_buf, r, first_core)
-
-    def finish(r):
-        weigh(theirs, *softened[r], k_buf, r)
+    def exponents(r):
+        weights[r], stats[0] = soften(s_buf, r, first_core, stats[0])
+
+    def numerators(r):
+        weigh(theirs, weights[r], k_buf, r)
 
     for copy in small:
         copy.wait()
-    for copy in large:
-        copy.wait()
-    for stage in (score, weights_of, finish):
-        for r in range(rows):
-            stage(r)
+    parts = [range(4), range(4, rows)]
+    for step in range(4):
+        if step < 2:
+            for r in parts[step]:
+                large[r].wait()
+        for part, stage in ((step - 2, numerators), (step - 1, exponents), (step, score)):
+            if 0 <= part < 2:
+                for r in parts[part]:
+                    stage(r)
+    theirs[pl.ds(rows * TILES, heads // 2, stride=rows * TILES + 1), :] = stats[0]
 
 
 def attend_mine(s_buf, k_buf, mine):
-    first_core = lax.rem(lax.axis_index("kv"), 2) == 0
-    softened = [soften_one(s_buf, r, jnp.logical_not(first_core)) for r in range(k_buf.shape[0])]
-    for r, pair in enumerate(softened):
-        weigh(mine, *pair, k_buf, r)
+    finish(mine, s_buf, k_buf, lax.rem(lax.axis_index("kv"), 2) == 1)
 
 
 def merge_cores(rows, order, got, mine, merged):
-    block = rows * (TILES + 1)
     sent = rows * TILES + 1
-    lane = lane_of(rows)
-    first_half = lane < HALF
-    diagonal = lax.rem(lane, HALF) == lax.broadcasted_iota(jnp.int32, (rows, LANES), 0)
+    chips = len(order)
+    stats = [ref[pl.ds(rows * TILES, chips, stride=sent), :] for ref in (got, mine)]
+    top = jnp.maximum(*stats)
+    weights = [jnp.exp(s - top) for s in stats]
+    total = sum(pltpu.roll(s, HALF, 1) * w for s, w in zip(stats, weights))
+    both = jnp.where(lane_of(chips) < HALF, top, pltpu.roll(total, HALF, 1))
+    columns = [jnp.transpose(w)[:rows] for w in weights]
     for slot, q in enumerate(order):
-        stats = [ref[q * block + rows * TILES : (q + 1) * block, :] for ref in (got, mine)]
-        tops = [jnp.where(first_half, s, pltpu.roll(s, HALF, 1)) for s in stats]
-        top = jnp.maximum(*tops)
-        weights = [jnp.exp(t - top) for t in tops]
+        factors = [jnp.broadcast_to(c[:, q : q + 1], (rows, LANES)) for c in columns]
         for t in range(TILES):
-            at = pl.ds(q * block + t * rows, rows)
+            at = pl.ds(q * sent + t * rows, rows)
             merged[slot * sent + t * rows : slot * sent + (t + 1) * rows, :] = (
-                got[at, :] * weights[0] + mine[at, :] * weights[1]
+                got[at, :] * factors[0] + mine[at, :] * factors[1]
             )
-        both = jnp.where(first_half, top, stats[0] * weights[0] + stats[1] * weights[1])
-        merged[slot * sent + TILES * rows : (slot + 1) * sent, :] = jnp.sum(
-            jnp.where(diagonal, both, 0.0), axis=0, keepdims=True
-        )
+        merged[slot * sent + TILES * rows : (slot + 1) * sent, :] = both[q : q + 1]
 
 
 def project(rows, order, got, value_up, out_proj, theirs, mine):
@@ -127,11 +140,13 @@
     core = lax.rem(lax.axis_index("kv"), 2)
     stats = got[pl.ds(TILES * rows, chips, stride=sent), :]
     weight = jnp.exp(stats - jnp.max(stats, axis=0, keepdims=True))
-    total = jnp.sum(weight * pltpu.roll(stats, HALF, 1), axis=0, keepdims=True)
-    coefficient = jnp.transpose(jnp.where(lane_of(chips) < rows, weight / total, 0.0))[:rows]
+    column = jnp.transpose(weight)[:rows]
+    total = jnp.sum(
+        jnp.transpose(weight * pltpu.roll(stats, HALF, 1))[:rows], axis=1, keepdims=True
+    )
     combined = [jnp.zeros((rows, LANES), jnp.float32) for _ in range(TILES)]
     for j in range(chips):
-        factor = jnp.broadcast_to(coefficient[:, j : j + 1], (rows, LANES))
+        factor = jnp.broadcast_to(column[:, j : j + 1], (rows, LANES))
         for t in range(TILES):
             combined[t] += factor * got[j * sent + t * rows : j * sent + (t + 1) * rows, :]
     head_values = jnp.dot(
@@ -140,7 +155,7 @@
         preferred_element_type=jnp.float32,
     )
     projection = jnp.dot(
-        head_values.astype(jnp.bfloat16), out_proj[...], preferred_element_type=jnp.float32
+        (head_values / total).astype(jnp.bfloat16), out_proj[...], preferred_element_type=jnp.float32
     )
     spare = LANES - features
     lane = lane_of(rows)
@@ -191,9 +206,8 @@
     params = pltpu.CompilerParams(vmem_limit_bytes=8 * 2**20)
     f32 = jnp.float32
 
-    block = rows * (TILES + 1)
     sent = rows * TILES + 1
-    partials = jax.ShapeDtypeStruct((chips * block, LANES), f32)
+    partials = jax.ShapeDtypeStruct((chips * sent, LANES), f32)
     theirs, scores, held = pl.pallas_call(
         attend_theirs,
         out_shape=[
@@ -220,7 +234,7 @@
     )(scores, held)
     merged = pl.pallas_call(
         lambda *refs: merge_cores(rows, order, *refs),
-        out_shape=jax.ShapeDtypeStruct((chips * sent, LANES), f32),
+        out_shape=partials,
         in_specs=vmem_specs(2),
         out_specs=vmem_specs(1)[0],
         compiler_params=params,

time: 51.9 us -> 51.4 us (level)
  transfers between devices with their start and end apart: 1 -> 1, of which waited for: 1 -> 1; matrix products, arithmetic and copies ran while one was open for 0% -> 0% of each run, Pallas kernels for 2% -> 1%
where the time goes in v5:
time: 51.4 us; the launch traced here: 51.2 us
  blocking collectives  36.2 us (70%)
  starting transfers between devices  8.79 us (17%)
  Pallas kernels  5.39 us (10%)
  waiting for transfers between devices  0.77 us (1%)
    all_to_all x1, blocking collectives, on_device(): lax.all_to_all(merged.reshape(chips, 1, sent * LANES), 'kv', 0, 0, axis_i...  20.8 us
    all_to_all x1, blocking collectives, on_device(): lax.all_to_all(summed.reshape(chips, 1, (rows - 1) * LANES), 'kv', 0, 0,...  12 us
    ppermute x1, starting transfers between devices, core_swap(): return lax.ppermute(x, 'kv', [(i, i ^ 1) for i in range(kv)])  8.79 us
    all_gather x1, blocking collectives, on_device(): lax.all_gather(theirs, 'kv', axis_index_groups=[[2 * i, 2 * i + 1] for i...  3.42 us
    pallas_call x1, Pallas kernels, on_device(): pl.pallas_call(attend_theirs, out_shape=[partials, jax.ShapeDtypeStruct((...  2.82 us
  transfers between devices with their start and end apart: 1, of which 1 were waited for; matrix products, arithmetic and copies ran while one was open for 0% of the time, Pallas kernels for 1%

profile of v5, /device:TPU:1, one launch (start us, length us, event | category | flops | bytes accessed | tf_op | source)
XLA Modules:
  0.0 51.2 jit_solution(171256180492668158)
XLA Ops:
  0.0 2.8 %shard_map.55 = (f32[1056,128]{1,0:T(8,128)S(1)}, f32[8,2,64,128]{3,2,1,0:T(8,128)S(1)}, bf16[8,576,256]{2,1,0:T(8,128)(2,1)S(1)}) custom-call(s32[8]{0:T(128)} %lengths.1, bf16[8,64,576]{2,1,0:T(8,128)(2,1)} %queries.1, bf16[8,576,256]{2,1,0:T(8,128)(2,1)} %bitcast.11), custom_call_target="tpu_custom_call" | custom-call | tf_op jit(solution)/shard_map/pallas_call | solution.py:211
  2.8 8.8 %collective-permute-start = (f32[1056,128]{1,0:T(8,128)S(1)}, f32[1056,128]{1,0:T(8,128)S(1)}, u32[]{:S(2)}, u32[]{:S(2)}) collective-permute-start(f32[1056,128]{1,0:T(8,128)S(1)} %get-tuple-element.10), channel_id=1, source_target_pairs={{0,1},{1,0},{2,3},{3,2},{4,5},{5,4},{6,7},{7,6},{8,9},{9,8},{10,11... | collective-permute-start | bytes 1622024 | tf_op jit(solution)/shard_map/ppermute | solution.py:192
  11.6 0.0 copy-start
  11.6 0.0 copy-start.1
  11.7 0.7 %shard_map.56.refs_1_ = f32[1056,128]{1,0:T(8,128)S(1)} custom-call(f32[8,2,64,128]{3,2,1,0:T(8,128)S(1)} %get-tuple-element.11.s_buf, bf16[8,576,256]{2,1,0:T(8,128)(2,1)S(1)} %get-tuple-element.12.k_buf), custom_call_target="tpu_custom_call" | custom-call | tf_op jit(solution)/shard_map/pallas_call | solution.py:228
  12.4 0.8 %collective-permute-done.refs_0_ = f32[1056,128]{1,0:T(8,128)S(1)} collective-permute-done((f32[1056,128]{1,0:T(8,128)S(1)}, f32[1056,128]{1,0:T(8,128)S(1)}, u32[]{:S(2)}, u32[]{:S(2)}) %collective-permute-start) | collective-permute-done | bytes 540704 | tf_op jit(solution)/shard_map/ppermute | solution.py:192
  13.2 0.3 shard_map.57
  13.4 20.8 %all_to_all.10 = f32[32,1,4224]{2,1,0:T(1,128)S(1)} all-to-all(f32[32,1,4224]{2,1,0:T(1,128)S(1)} %bitcast.7), channel_id=1, replica_groups={{38,40,42,44,46,48,50,52,54,56,58,60,62,0,2,4,6,8,10,12,14,16,18,20,22,..., dimensions={0} | all-to-all | bytes 1081344 | tf_op jit(solution)/shard_map/all_to_all | solution.py:242
  34.2 0.0 copy-done
  34.3 0.0 copy-done.1
  34.3 0.9 %shard_map.58 = (f32[224,128]{1,0:T(8,128)S(1)}, f32[224,128]{1,0:T(8,128)S(1)}) custom-call(f32[1056,128]{1,0:T(8,128)S(1)} %bitcast.6, bf16[1,512,128]{2,1,0:T(8,128)(2,1)S(1)} %copy-done.1, bf16[128,7168]{1,0:T(8,128)(2,1)S(1)} %copy-done), custom_call_target="tpu_custom_call" | custom-call | tf_op jit(solution)/shard_map/pallas_call | solution.py:246
  35.1 3.4 %all-gather = f32[448,128]{1,0:T(8,128)S(1)} all-gather(f32[224,128]{1,0:T(8,128)S(1)} %get-tuple-element.13), channel_id=2, replica_groups={{0,1},{2,3},{4,5},{6,7},{8,9},{10,11},{12,13},{14,15},{16,17},{18,19},{..., dimensions={0}, use_global_device_ids=true | all-gather | bytes 344064 | tf_op jit(solution)/shard_map/all_gather | solution.py:253
  38.5 12.0 %all_to_all.11 = f32[32,1,896]{2,1,0:T(1,128)S(1)} all-to-all(f32[32,1,896]{2,1,0:T(1,128)S(1)} %bitcast.9), channel_id=1, replica_groups={{38,40,42,44,46,48,50,52,54,56,58,60,62,0,2,4,6,8,10,12,14,16,18,20,22,..., dimensions={0} | all-to-all | bytes 229376 | tf_op jit(solution)/shard_map/all_to_all | solution.py:263
  50.5 0.7 %shard_map.60 = bf16[8,112]{1,0:T(8,128)(2,1)} custom-call(f32[224,128]{1,0:T(8,128)S(1)} %bitcast.10), custom_call_target="tpu_custom_call" | custom-call | tf_op jit(solution)/shard_map/pallas_call | solution.py:266
  (1 shorter events, 0.0 us)
Async XLA Ops:
  2.8 10.3 %collective-permute-start = (f32[1056,128]{1,0:T(8,128)S(1)}, f32[1056,128]{1,0:T(8,128)S(1)}, u32[]{:S(2)}, u32[]{:S(2)}) collective-permute-start(f32[1056,128]{1,0:T(8,128)S(1)} %get-tuple-element.10), channel_id=1, source_target_pairs={{0,1},{1,0},{2,3},{3,2},{4,5},{5,4},{6,7},{7,6},{8,9},{9,8},{10,11... | collective-permute-start | bytes 1622024 | tf_op jit(solution)/shard_map/ppermute | solution.py:192
  11.6 22.6 %copy-start = (bf16[128,7168]{1,0:T(8,128)(2,1)S(1)}, bf16[128,7168]{1,0:T(8,128)(2,1)}, u32[]{:S(2)}) copy-start(bf16[128,7168]{1,0:T(8,128)(2,1)} %refs_2_.1) | copy-start | bytes 5505028
  11.6 22.6 %copy-start.1 = (bf16[1,512,128]{2,1,0:T(8,128)(2,1)S(1)}, bf16[1,512,128]{2,1,0:T(8,128)(2,1)}, u32[]{:S(2)}) copy-start(bf16[1,512,128]{2,1,0:T(8,128)(2,1)} %refs_1_.1) | copy-start | bytes 393220

commit v6 on v5

--- a/solution.py
+++ b/solution.py
@@ -140,15 +140,22 @@
     core = lax.rem(lax.axis_index("kv"), 2)
     stats = got[pl.ds(TILES * rows, chips, stride=sent), :]
     weight = jnp.exp(stats - jnp.max(stats, axis=0, keepdims=True))
-    column = jnp.transpose(weight)[:rows]
-    total = jnp.sum(
-        jnp.transpose(weight * pltpu.roll(stats, HALF, 1))[:rows], axis=1, keepdims=True
-    )
-    combined = [jnp.zeros((rows, LANES), jnp.float32) for _ in range(TILES)]
-    for j in range(chips):
-        factor = jnp.broadcast_to(column[:, j : j + 1], (rows, LANES))
-        for t in range(TILES):
-            combined[t] += factor * got[j * sent + t * rows : j * sent + (t + 1) * rows, :]
+    total = jnp.sum(weight * pltpu.roll(stats, HALF, 1), axis=0, keepdims=True)
+    total = jnp.transpose(jnp.broadcast_to(total, (rows, LANES)))[:rows, :1]
+    combined = [
+        jnp.concatenate(
+            [
+                jnp.sum(
+                    got[pl.ds(t * rows + r, chips, stride=sent), :] * weight[:, r : r + 1],
+                    axis=0,
+                    keepdims=True,
+                )
+                for r in range(rows)
+            ],
+            axis=0,
+        )
+        for t in range(TILES)
+    ]
     head_values = jnp.dot(
         jnp.concatenate(combined, axis=1).astype(jnp.bfloat16),
         value_up[0],
@@ -192,8 +199,7 @@
     return lax.ppermute(x, "kv", [(i, i ^ 1) for i in range(kv)])
 
 
-def chip_order(chips):
-    first = 19 % chips
+def chips_from(first, chips):
     return [(first + i) % chips for i in range(chips)]
 
 
@@ -201,8 +207,8 @@
     rows, heads, width = queries.shape
     shard_len = latent_cache.shape[1]
     chips = kv // 2
-    order = chip_order(chips)
-    same_core = [[2 * i + c for i in order] for c in range(2)]
+    orders = [chips_from(first, chips) for first in (26, 19)]
+    same_core = [[[2 * i + c for i in order] for c in range(2)] for order in orders]
     params = pltpu.CompilerParams(vmem_limit_bytes=8 * 2**20)
     f32 = jnp.float32
 
@@ -233,18 +239,18 @@
         compiler_params=params,
     )(scores, held)
     merged = pl.pallas_call(
-        lambda *refs: merge_cores(rows, order, *refs),
+        lambda *refs: merge_cores(rows, orders[0], *refs),
         out_shape=partials,
         in_specs=vmem_specs(2),
         out_specs=vmem_specs(1)[0],
         compiler_params=params,
     )(got, mine)
     got = lax.all_to_all(
-        merged.reshape(chips, 1, sent * LANES), "kv", 0, 0, axis_index_groups=same_core
+        merged.reshape(chips, 1, sent * LANES), "kv", 0, 0, axis_index_groups=same_core[0]
     ).reshape(chips * sent, LANES)
     features = jax.ShapeDtypeStruct((chips * (rows - 1), LANES), f32)
     theirs, mine = pl.pallas_call(
-        lambda *refs: project(rows, order, *refs),
+        lambda *refs: project(rows, orders[1], *refs),
         out_shape=[features] * 2,
         in_specs=vmem_specs(3),
         out_specs=vmem_specs(2),
@@ -261,7 +267,7 @@
         compiler_params=params,
     )(both, mine)
     parts = lax.all_to_all(
-        summed.reshape(chips, 1, (rows - 1) * LANES), "kv", 0, 0, axis_index_groups=same_core
+        summed.reshape(chips, 1, (rows - 1) * LANES), "kv", 0, 0, axis_index_groups=same_core[1]
     ).reshape(chips * (rows - 1), LANES)
     return pl.pallas_call(
         add_up,

time: 51.4 us -> 51.4 us (level)
  no operation moved by 1% of the time
where the time goes in v6:
time: 51.4 us; the launch traced here: 51.1 us
  blocking collectives  36.2 us (70%)
  starting transfers between devices  8.79 us (17%)
  Pallas kernels  5.31 us (10%)
  waiting for transfers between devices  0.77 us (1%)
    all_to_all x1, blocking collectives, on_device(): lax.all_to_all(merged.reshape(chips, 1, sent * LANES), 'kv', 0, 0, axis_i...  20.4 us
    all_to_all x1, blocking collectives, on_device(): lax.all_to_all(summed.reshape(chips, 1, (rows - 1) * LANES), 'kv', 0, 0,...  12.3 us
    ppermute x1, starting transfers between devices, core_swap(): return lax.ppermute(x, 'kv', [(i, i ^ 1) for i in range(kv)])  8.79 us
    all_gather x1, blocking collectives, on_device(): lax.all_gather(theirs, 'kv', axis_index_groups=[[2 * i, 2 * i + 1] for i...  3.58 us
    pallas_call x1, Pallas kernels, on_device(): pl.pallas_call(attend_theirs, out_shape=[partials, jax.ShapeDtypeStruct((...  2.82 us
  transfers between devices with their start and end apart: 1, of which 1 were waited for; matrix products, arithmetic and copies ran while one was open for 0% of the time, Pallas kernels for 1%

profile of v6, /device:TPU:1, one launch (start us, length us, event | category | flops | bytes accessed | tf_op | source)
XLA Modules:
  0.0 51.1 jit_solution(17334299510391254142)
XLA Ops:
  0.0 2.8 %shard_map.55 = (f32[1056,128]{1,0:T(8,128)S(1)}, f32[8,2,64,128]{3,2,1,0:T(8,128)S(1)}, bf16[8,576,256]{2,1,0:T(8,128)(2,1)S(1)}) custom-call(s32[8]{0:T(128)} %lengths.1, bf16[8,64,576]{2,1,0:T(8,128)(2,1)} %queries.1, bf16[8,576,256]{2,1,0:T(8,128)(2,1)} %bitcast.11), custom_call_target="tpu_custom_call" | custom-call | tf_op jit(solution)/shard_map/pallas_call | solution.py:217
  2.8 8.8 %collective-permute-start = (f32[1056,128]{1,0:T(8,128)S(1)}, f32[1056,128]{1,0:T(8,128)S(1)}, u32[]{:S(2)}, u32[]{:S(2)}) collective-permute-start(f32[1056,128]{1,0:T(8,128)S(1)} %get-tuple-element.10), channel_id=1, source_target_pairs={{0,1},{1,0},{2,3},{3,2},{4,5},{5,4},{6,7},{7,6},{8,9},{9,8},{10,11... | collective-permute-start | bytes 1622024 | tf_op jit(solution)/shard_map/ppermute | solution.py:199
  11.6 0.0 copy-start
  11.6 0.0 copy-start.1
  11.7 0.7 %shard_map.56.refs_1_ = f32[1056,128]{1,0:T(8,128)S(1)} custom-call(f32[8,2,64,128]{3,2,1,0:T(8,128)S(1)} %get-tuple-element.11.s_buf, bf16[8,576,256]{2,1,0:T(8,128)(2,1)S(1)} %get-tuple-element.12.k_buf), custom_call_target="tpu_custom_call" | custom-call | tf_op jit(solution)/shard_map/pallas_call | solution.py:234
  12.4 0.8 %collective-permute-done.refs_0_ = f32[1056,128]{1,0:T(8,128)S(1)} collective-permute-done((f32[1056,128]{1,0:T(8,128)S(1)}, f32[1056,128]{1,0:T(8,128)S(1)}, u32[]{:S(2)}, u32[]{:S(2)}) %collective-permute-start) | collective-permute-done | bytes 540704 | tf_op jit(solution)/shard_map/ppermute | solution.py:199
  13.2 0.3 shard_map.57
  13.4 20.4 %all_to_all.10 = f32[32,1,4224]{2,1,0:T(1,128)S(1)} all-to-all(f32[32,1,4224]{2,1,0:T(1,128)S(1)} %bitcast.7), channel_id=1, replica_groups={{52,54,56,58,60,62,0,2,4,6,8,10,12,14,16,18,20,22,24,26,28,30,32,34,36,..., dimensions={0} | all-to-all | bytes 1081344 | tf_op jit(solution)/shard_map/all_to_all | solution.py:248
  33.8 0.0 copy-done
  33.8 0.0 copy-done.1
  33.8 0.8 %shard_map.58 = (f32[224,128]{1,0:T(8,128)S(1)}, f32[224,128]{1,0:T(8,128)S(1)}) custom-call(f32[1056,128]{1,0:T(8,128)S(1)} %bitcast.6, bf16[1,512,128]{2,1,0:T(8,128)(2,1)S(1)} %copy-done.1, bf16[128,7168]{1,0:T(8,128)(2,1)S(1)} %copy-done), custom_call_target="tpu_custom_call" | custom-call | tf_op jit(solution)/shard_map/pallas_call | solution.py:252
  34.6 3.6 %all-gather = f32[448,128]{1,0:T(8,128)S(1)} all-gather(f32[224,128]{1,0:T(8,128)S(1)} %get-tuple-element.13), channel_id=2, replica_groups={{0,1},{2,3},{4,5},{6,7},{8,9},{10,11},{12,13},{14,15},{16,17},{18,19},{..., dimensions={0}, use_global_device_ids=true | all-gather | bytes 344064 | tf_op jit(solution)/shard_map/all_gather | solution.py:259
  38.2 12.3 %all_to_all.11 = f32[32,1,896]{2,1,0:T(1,128)S(1)} all-to-all(f32[32,1,896]{2,1,0:T(1,128)S(1)} %bitcast.9), channel_id=1, replica_groups={{38,40,42,44,46,48,50,52,54,56,58,60,62,0,2,4,6,8,10,12,14,16,18,20,22,..., dimensions={0} | all-to-all | bytes 229376 | tf_op jit(solution)/shard_map/all_to_all | solution.py:269
  50.5 0.7 %shard_map.60 = bf16[8,112]{1,0:T(8,128)(2,1)} custom-call(f32[224,128]{1,0:T(8,128)S(1)} %bitcast.10), custom_call_target="tpu_custom_call" | custom-call | tf_op jit(solution)/shard_map/pallas_call | solution.py:272
  (1 shorter events, 0.0 us)
Async XLA Ops:
  2.8 10.3 %collective-permute-start = (f32[1056,128]{1,0:T(8,128)S(1)}, f32[1056,128]{1,0:T(8,128)S(1)}, u32[]{:S(2)}, u32[]{:S(2)}) collective-permute-start(f32[1056,128]{1,0:T(8,128)S(1)} %get-tuple-element.10), channel_id=1, source_target_pairs={{0,1},{1,0},{2,3},{3,2},{4,5},{5,4},{6,7},{7,6},{8,9},{9,8},{10,11... | collective-permute-start | bytes 1622024 | tf_op jit(solution)/shard_map/ppermute | solution.py:199
  11.6 22.2 %copy-start = (bf16[128,7168]{1,0:T(8,128)(2,1)S(1)}, bf16[128,7168]{1,0:T(8,128)(2,1)}, u32[]{:S(2)}) copy-start(bf16[128,7168]{1,0:T(8,128)(2,1)} %refs_2_.1) | copy-start | bytes 5505028
  11.6 22.2 %copy-start.1 = (bf16[1,512,128]{2,1,0:T(8,128)(2,1)S(1)}, bf16[1,512,128]{2,1,0:T(8,128)(2,1)}, u32[]{:S(2)}) copy-start(bf16[1,512,128]{2,1,0:T(8,128)(2,1)} %refs_1_.1) | copy-start | bytes 393220

commit v7 on v6

--- a/solution.py
+++ b/solution.py
@@ -122,15 +122,23 @@
     weights = [jnp.exp(s - top) for s in stats]
     total = sum(pltpu.roll(s, HALF, 1) * w for s, w in zip(stats, weights))
     both = jnp.where(lane_of(chips) < HALF, top, pltpu.roll(total, HALF, 1))
-    columns = [jnp.transpose(w)[:rows] for w in weights]
-    for slot, q in enumerate(order):
-        factors = [jnp.broadcast_to(c[:, q : q + 1], (rows, LANES)) for c in columns]
+    spans, slot = [], 0
+    while slot < chips:
+        q = order[slot]
+        span = chips - q if slot == 0 else chips - slot
+        spans.append((q, slot, span))
+        slot += span
+    for r in range(rows):
+        columns = [jnp.broadcast_to(w[:, r : r + 1], (chips, LANES)) for w in weights]
         for t in range(TILES):
-            at = pl.ds(q * sent + t * rows, rows)
-            merged[slot * sent + t * rows : slot * sent + (t + 1) * rows, :] = (
-                got[at, :] * factors[0] + mine[at, :] * factors[1]
-            )
-        merged[slot * sent + TILES * rows : (slot + 1) * sent, :] = both[q : q + 1]
+            row = t * rows + r
+            for q, slot, span in spans:
+                at = pl.ds(q * sent + row, span, stride=sent)
+                merged[pl.ds(slot * sent + row, span, stride=sent), :] = (
+                    got[at, :] * columns[0][q : q + span] + mine[at, :] * columns[1][q : q + span]
+                )
+    for q, slot, span in spans:
+        merged[pl.ds((slot + 1) * sent - 1, span, stride=sent), :] = both[q : q + span]
 
 
 def project(rows, order, got, value_up, out_proj, theirs, mine):
@@ -186,9 +194,10 @@
 def add_up(got, out):
     rows, features = out.shape
     spare = LANES - features
-    total = got[pl.ds(0, rows - 1), :]
-    for j in range(1, got.shape[0] // (rows - 1)):
-        total += got[pl.ds(j * (rows - 1), rows - 1), :]
+    parts = [got[pl.ds(j, rows - 1), :] for j in range(0, got.shape[0], rows - 1)]
+    while len(parts) > 1:
+        parts = [sum(parts[i : i + 2]) for i in range(0, len(parts), 2)]
+    total = parts[0]
     last = [total[i : i + 1, features:] for i in reversed(range(rows - 1))]
     out[...] = jnp.concatenate(
         [total[:, :features], jnp.concatenate(last, axis=1)], axis=0

time: 51.4 us -> 51.3 us (level)
  no operation moved by 1% of the time
where the time goes in v7:
time: 51.3 us; the launch traced here: 51 us
  blocking collectives  36.2 us (71%)
  starting transfers between devices  8.79 us (17%)
  Pallas kernels  5.2 us (10%)
  waiting for transfers between devices  0.77 us (2%)
    all_to_all x1, blocking collectives, on_device(): lax.all_to_all(merged.reshape(chips, 1, sent * LANES), 'kv', 0, 0, axis_i...  20.4 us
    all_to_all x1, blocking collectives, on_device(): lax.all_to_all(summed.reshape(chips, 1, (rows - 1) * LANES), 'kv', 0, 0,...  12.3 us
    ppermute x1, starting transfers between devices, core_swap(): return lax.ppermute(x, 'kv', [(i, i ^ 1) for i in range(kv)])  8.79 us
    all_gather x1, blocking collectives, on_device(): lax.all_gather(theirs, 'kv', axis_index_groups=[[2 * i, 2 * i + 1] for i...  3.58 us
    pallas_call x1, Pallas kernels, on_device(): pl.pallas_call(attend_theirs, out_shape=[partials, jax.ShapeDtypeStruct((...  2.82 us
  transfers between devices with their start and end apart: 1, of which 1 were waited for; matrix products, arithmetic and copies ran while one was open for 0% of the time, Pallas kernels for 1%

profile of v7, /device:TPU:1, one launch (start us, length us, event | category | flops | bytes accessed | tf_op | source)
XLA Modules:
  0.0 51.0 jit_solution(8717680467465992535)
XLA Ops:
  0.0 2.8 %shard_map.55 = (f32[1056,128]{1,0:T(8,128)S(1)}, f32[8,2,64,128]{3,2,1,0:T(8,128)S(1)}, bf16[8,576,256]{2,1,0:T(8,128)(2,1)S(1)}) custom-call(s32[8]{0:T(128)} %lengths.1, bf16[8,64,576]{2,1,0:T(8,128)(2,1)} %queries.1, bf16[8,576,256]{2,1,0:T(8,128)(2,1)} %bitcast.11), custom_call_target="tpu_custom_call" | custom-call | tf_op jit(solution)/shard_map/pallas_call | solution.py:226
  2.8 8.8 %collective-permute-start = (f32[1056,128]{1,0:T(8,128)S(1)}, f32[1056,128]{1,0:T(8,128)S(1)}, u32[]{:S(2)}, u32[]{:S(2)}) collective-permute-start(f32[1056,128]{1,0:T(8,128)S(1)} %get-tuple-element.10), channel_id=1, source_target_pairs={{0,1},{1,0},{2,3},{3,2},{4,5},{5,4},{6,7},{7,6},{8,9},{9,8},{10,11... | collective-permute-start | bytes 1622024 | tf_op jit(solution)/shard_map/ppermute | solution.py:208
  11.6 0.0 copy-start
  11.6 0.0 copy-start.1
  11.7 0.7 %shard_map.56.refs_1_ = f32[1056,128]{1,0:T(8,128)S(1)} custom-call(f32[8,2,64,128]{3,2,1,0:T(8,128)S(1)} %get-tuple-element.11.s_buf, bf16[8,576,256]{2,1,0:T(8,128)(2,1)S(1)} %get-tuple-element.12.k_buf), custom_call_target="tpu_custom_call" | custom-call | tf_op jit(solution)/shard_map/pallas_call | solution.py:243
  12.4 0.8 %collective-permute-done.refs_0_ = f32[1056,128]{1,0:T(8,128)S(1)} collective-permute-done((f32[1056,128]{1,0:T(8,128)S(1)}, f32[1056,128]{1,0:T(8,128)S(1)}, u32[]{:S(2)}, u32[]{:S(2)}) %collective-permute-start) | collective-permute-done | bytes 540704 | tf_op jit(solution)/shard_map/ppermute | solution.py:208
  13.2 0.2 shard_map.57
  13.4 20.4 %all_to_all.10 = f32[32,1,4224]{2,1,0:T(1,128)S(1)} all-to-all(f32[32,1,4224]{2,1,0:T(1,128)S(1)} %bitcast.7), channel_id=1, replica_groups={{52,54,56,58,60,62,0,2,4,6,8,10,12,14,16,18,20,22,24,26,28,30,32,34,36,..., dimensions={0} | all-to-all | bytes 1081344 | tf_op jit(solution)/shard_map/all_to_all | solution.py:257
  33.7 0.0 copy-done
  33.7 0.0 copy-done.1
  33.7 0.8 %shard_map.58 = (f32[224,128]{1,0:T(8,128)S(1)}, f32[224,128]{1,0:T(8,128)S(1)}) custom-call(f32[1056,128]{1,0:T(8,128)S(1)} %bitcast.6, bf16[1,512,128]{2,1,0:T(8,128)(2,1)S(1)} %copy-done.1, bf16[128,7168]{1,0:T(8,128)(2,1)S(1)} %copy-done), custom_call_target="tpu_custom_call" | custom-call | tf_op jit(solution)/shard_map/pallas_call | solution.py:261
  34.5 3.6 %all-gather = f32[448,128]{1,0:T(8,128)S(1)} all-gather(f32[224,128]{1,0:T(8,128)S(1)} %get-tuple-element.13), channel_id=2, replica_groups={{0,1},{2,3},{4,5},{6,7},{8,9},{10,11},{12,13},{14,15},{16,17},{18,19},{..., dimensions={0}, use_global_device_ids=true | all-gather | bytes 344064 | tf_op jit(solution)/shard_map/all_gather | solution.py:268
  38.1 12.3 %all_to_all.11 = f32[32,1,896]{2,1,0:T(1,128)S(1)} all-to-all(f32[32,1,896]{2,1,0:T(1,128)S(1)} %bitcast.9), channel_id=1, replica_groups={{38,40,42,44,46,48,50,52,54,56,58,60,62,0,2,4,6,8,10,12,14,16,18,20,22,..., dimensions={0} | all-to-all | bytes 229376 | tf_op jit(solution)/shard_map/all_to_all | solution.py:278
  50.4 0.7 %shard_map.60 = bf16[8,112]{1,0:T(8,128)(2,1)} custom-call(f32[224,128]{1,0:T(8,128)S(1)} %bitcast.10), custom_call_target="tpu_custom_call" | custom-call | tf_op jit(solution)/shard_map/pallas_call | solution.py:281
  (1 shorter events, 0.0 us)
Async XLA Ops:
  2.8 10.3 %collective-permute-start = (f32[1056,128]{1,0:T(8,128)S(1)}, f32[1056,128]{1,0:T(8,128)S(1)}, u32[]{:S(2)}, u32[]{:S(2)}) collective-permute-start(f32[1056,128]{1,0:T(8,128)S(1)} %get-tuple-element.10), channel_id=1, source_target_pairs={{0,1},{1,0},{2,3},{3,2},{4,5},{5,4},{6,7},{7,6},{8,9},{9,8},{10,11... | collective-permute-start | bytes 1622024 | tf_op jit(solution)/shard_map/ppermute | solution.py:208
  11.6 22.1 %copy-start = (bf16[128,7168]{1,0:T(8,128)(2,1)S(1)}, bf16[128,7168]{1,0:T(8,128)(2,1)}, u32[]{:S(2)}) copy-start(bf16[128,7168]{1,0:T(8,128)(2,1)} %refs_2_.1) | copy-start | bytes 5505028
  11.6 22.1 %copy-start.1 = (bf16[1,512,128]{2,1,0:T(8,128)(2,1)S(1)}, bf16[1,512,128]{2,1,0:T(8,128)(2,1)}, u32[]{:S(2)}) copy-start(bf16[1,512,128]{2,1,0:T(8,128)(2,1)} %refs_1_.1) | copy-start | bytes 393220

commit v8 on v6

--- a/solution.py
+++ b/solution.py
@@ -123,6 +123,8 @@
     total = sum(pltpu.roll(s, HALF, 1) * w for s, w in zip(stats, weights))
     both = jnp.where(lane_of(chips) < HALF, top, pltpu.roll(total, HALF, 1))
     columns = [jnp.transpose(w)[:rows] for w in weights]
+    turned = jnp.concatenate([both[order[0] :], both[: order[0]]], axis=0)
+    merged[pl.ds(rows * TILES, chips, stride=sent), :] = turned
     for slot, q in enumerate(order):
         factors = [jnp.broadcast_to(c[:, q : q + 1], (rows, LANES)) for c in columns]
         for t in range(TILES):
@@ -130,7 +132,6 @@
             merged[slot * sent + t * rows : slot * sent + (t + 1) * rows, :] = (
                 got[at, :] * factors[0] + mine[at, :] * factors[1]
             )
-        merged[slot * sent + TILES * rows : (slot + 1) * sent, :] = both[q : q + 1]
 
 
 def project(rows, order, got, value_up, out_proj, theirs, mine):
@@ -180,15 +181,19 @@
 
 
 def add_other(both, mine, out):
-    out[...] = mine[...] + both[1 - lax.rem(lax.axis_index("kv"), 2)]
+    at = pl.ds(0, out.shape[0])
+    out[...] = mine[at, :] + both[1 - lax.rem(lax.axis_index("kv"), 2), at, :]
 
 
 def add_up(got, out):
     rows, features = out.shape
     spare = LANES - features
-    total = got[pl.ds(0, rows - 1), :]
-    for j in range(1, got.shape[0] // (rows - 1)):
-        total += got[pl.ds(j * (rows - 1), rows - 1), :]
+    count = got.shape[0]
+    parts = [got[pl.ds(j, rows - 1), :] for j in range(0, count - rows + 1, rows - 1)]
+    parts.append(got[pl.ds(count - rows, rows), :][1:])
+    while len(parts) > 1:
+        parts = [sum(parts[i : i + 2]) for i in range(0, len(parts), 2)]
+    total = parts[0]
     last = [total[i : i + 1, features:] for i in reversed(range(rows - 1))]
     out[...] = jnp.concatenate(
         [total[:, :features], jnp.concatenate(last, axis=1)], axis=0
@@ -248,7 +253,8 @@
     got = lax.all_to_all(
         merged.reshape(chips, 1, sent * LANES), "kv", 0, 0, axis_index_groups=same_core[0]
     ).reshape(chips * sent, LANES)
-    features = jax.ShapeDtypeStruct((chips * (rows - 1), LANES), f32)
+    packed = jax.ShapeDtypeStruct((chips * (rows - 1), LANES), f32)
+    features = jax.ShapeDtypeStruct((chips * (rows - 1) + rows, LANES), f32)
     theirs, mine = pl.pallas_call(
         lambda *refs: project(rows, orders[1], *refs),
         out_shape=[features] * 2,
@@ -261,7 +267,7 @@
     )
     summed = pl.pallas_call(
         add_other,
-        out_shape=features,
+        out_shape=packed,
         in_specs=vmem_specs(2),
         out_specs=vmem_specs(1)[0],
         compiler_params=params,

time: 51.4 us -> 51.4 us (level)
  no operation moved by 1% of the time
where the time goes in v8:
time: 51.4 us; the launch traced here: 51.1 us
  blocking collectives  36.2 us (70%)
  starting transfers between devices  8.79 us (17%)
  Pallas kernels  5.29 us (10%)
  waiting for transfers between devices  0.77 us (1%)
    all_to_all x1, blocking collectives, on_device(): lax.all_to_all(merged.reshape(chips, 1, sent * LANES), 'kv', 0, 0, axis_i...  20.4 us
    all_to_all x1, blocking collectives, on_device(): lax.all_to_all(summed.reshape(chips, 1, (rows - 1) * LANES), 'kv', 0, 0,...  12.3 us
    ppermute x1, starting transfers between devices, core_swap(): return lax.ppermute(x, 'kv', [(i, i ^ 1) for i in range(kv)])  8.79 us
    all_gather x1, blocking collectives, on_device(): lax.all_gather(theirs, 'kv', axis_index_groups=[[2 * i, 2 * i + 1] for i...  3.59 us
    pallas_call x1, Pallas kernels, on_device(): pl.pallas_call(attend_theirs, out_shape=[partials, jax.ShapeDtypeStruct((...  2.82 us
  transfers between devices with their start and end apart: 1, of which 1 were waited for; matrix products, arithmetic and copies ran while one was open for 0% of the time, Pallas kernels for 1%

profile of v8, /device:TPU:1, one launch (start us, length us, event | category | flops | bytes accessed | tf_op | source)
XLA Modules:
  0.0 51.1 jit_solution(12901773220150980369)
XLA Ops:
  0.0 2.8 %shard_map.55 = (f32[1056,128]{1,0:T(8,128)S(1)}, f32[8,2,64,128]{3,2,1,0:T(8,128)S(1)}, bf16[8,576,256]{2,1,0:T(8,128)(2,1)S(1)}) custom-call(s32[8]{0:T(128)} %lengths.1, bf16[8,64,576]{2,1,0:T(8,128)(2,1)} %queries.1, bf16[8,576,256]{2,1,0:T(8,128)(2,1)} %bitcast.11), custom_call_target="tpu_custom_call" | custom-call | tf_op jit(solution)/shard_map/pallas_call | solution.py:222
  2.8 8.8 %collective-permute-start = (f32[1056,128]{1,0:T(8,128)S(1)}, f32[1056,128]{1,0:T(8,128)S(1)}, u32[]{:S(2)}, u32[]{:S(2)}) collective-permute-start(f32[1056,128]{1,0:T(8,128)S(1)} %get-tuple-element.10), channel_id=1, source_target_pairs={{0,1},{1,0},{2,3},{3,2},{4,5},{5,4},{6,7},{7,6},{8,9},{9,8},{10,11... | collective-permute-start | bytes 1622024 | tf_op jit(solution)/shard_map/ppermute | solution.py:204
  11.6 0.0 copy-start
  11.6 0.0 copy-start.1
  11.7 0.7 %shard_map.56.refs_1_ = f32[1056,128]{1,0:T(8,128)S(1)} custom-call(f32[8,2,64,128]{3,2,1,0:T(8,128)S(1)} %get-tuple-element.11.s_buf, bf16[8,576,256]{2,1,0:T(8,128)(2,1)S(1)} %get-tuple-element.12.k_buf), custom_call_target="tpu_custom_call" | custom-call | tf_op jit(solution)/shard_map/pallas_call | solution.py:239
  12.4 0.8 %collective-permute-done.refs_0_ = f32[1056,128]{1,0:T(8,128)S(1)} collective-permute-done((f32[1056,128]{1,0:T(8,128)S(1)}, f32[1056,128]{1,0:T(8,128)S(1)}, u32[]{:S(2)}, u32[]{:S(2)}) %collective-permute-start) | collective-permute-done | bytes 540704 | tf_op jit(solution)/shard_map/ppermute | solution.py:204
  13.2 0.3 shard_map.57
  13.4 20.4 %all_to_all.10 = f32[32,1,4224]{2,1,0:T(1,128)S(1)} all-to-all(f32[32,1,4224]{2,1,0:T(1,128)S(1)} %bitcast.7), channel_id=1, replica_groups={{52,54,56,58,60,62,0,2,4,6,8,10,12,14,16,18,20,22,24,26,28,30,32,34,36,..., dimensions={0} | all-to-all | bytes 1081344 | tf_op jit(solution)/shard_map/all_to_all | solution.py:253
  33.8 0.0 copy-done
  33.8 0.0 copy-done.1
  33.8 0.8 %shard_map.58 = (f32[232,128]{1,0:T(8,128)S(1)}, f32[232,128]{1,0:T(8,128)S(1)}) custom-call(f32[1056,128]{1,0:T(8,128)S(1)} %bitcast.6, bf16[1,512,128]{2,1,0:T(8,128)(2,1)S(1)} %copy-done.1, bf16[128,7168]{1,0:T(8,128)(2,1)S(1)} %copy-done), custom_call_target="tpu_custom_call" | custom-call | tf_op jit(solution)/shard_map/pallas_call | solution.py:258
  34.6 3.6 %all-gather = f32[464,128]{1,0:T(8,128)S(1)} all-gather(f32[232,128]{1,0:T(8,128)S(1)} %get-tuple-element.13), channel_id=2, replica_groups={{0,1},{2,3},{4,5},{6,7},{8,9},{10,11},{12,13},{14,15},{16,17},{18,19},{..., dimensions={0}, use_global_device_ids=true | all-gather | bytes 356352 | tf_op jit(solution)/shard_map/all_gather | solution.py:265
  38.2 12.3 %all_to_all.11 = f32[32,1,896]{2,1,0:T(1,128)S(1)} all-to-all(f32[32,1,896]{2,1,0:T(1,128)S(1)} %bitcast.9), channel_id=1, replica_groups={{38,40,42,44,46,48,50,52,54,56,58,60,62,0,2,4,6,8,10,12,14,16,18,20,22,..., dimensions={0} | all-to-all | bytes 229376 | tf_op jit(solution)/shard_map/all_to_all | solution.py:275
  50.5 0.7 %shard_map.60 = bf16[8,112]{1,0:T(8,128)(2,1)} custom-call(f32[224,128]{1,0:T(8,128)S(1)} %bitcast.10), custom_call_target="tpu_custom_call" | custom-call | tf_op jit(solution)/shard_map/pallas_call | solution.py:278
  (1 shorter events, 0.0 us)
Async XLA Ops:
  2.8 10.3 %collective-permute-start = (f32[1056,128]{1,0:T(8,128)S(1)}, f32[1056,128]{1,0:T(8,128)S(1)}, u32[]{:S(2)}, u32[]{:S(2)}) collective-permute-start(f32[1056,128]{1,0:T(8,128)S(1)} %get-tuple-element.10), channel_id=1, source_target_pairs={{0,1},{1,0},{2,3},{3,2},{4,5},{5,4},{6,7},{7,6},{8,9},{9,8},{10,11... | collective-permute-start | bytes 1622024 | tf_op jit(solution)/shard_map/ppermute | solution.py:204
  11.6 22.2 %copy-start = (bf16[128,7168]{1,0:T(8,128)(2,1)S(1)}, bf16[128,7168]{1,0:T(8,128)(2,1)}, u32[]{:S(2)}) copy-start(bf16[128,7168]{1,0:T(8,128)(2,1)} %refs_2_.1) | copy-start | bytes 5505028
  11.6 22.2 %copy-start.1 = (bf16[1,512,128]{2,1,0:T(8,128)(2,1)S(1)}, bf16[1,512,128]{2,1,0:T(8,128)(2,1)}, u32[]{:S(2)}) copy-start(bf16[1,512,128]{2,1,0:T(8,128)(2,1)} %refs_1_.1) | copy-start | bytes 393220

commit v9 on v8

--- a/solution.py
+++ b/solution.py
@@ -26,7 +26,7 @@
     return lax.broadcasted_iota(jnp.int32, (rows, LANES), 1)
 
 
-def soften(s_buf, r, odd_wanted, stats):
+def soften(s_buf, r, odd_wanted, stats, first):
     pairs = s_buf.shape[2] // 2
     even, odd = [
         jnp.concatenate(
@@ -35,6 +35,7 @@
         for parity in range(2)
     ]
     part = jnp.where(odd_wanted, odd, even)
+    part = jnp.concatenate([part[first:], part[:first]], axis=0)
     top = jnp.max(part, axis=1, keepdims=True)
     exponent = jnp.where(part > 0.5 * masked_value, jnp.exp(part - top), 0.0)
     lane = lane_of(pairs)
@@ -55,20 +56,20 @@
         ]
 
 
-def finish(out, s_buf, k_buf, odd_wanted):
+def finish(out, s_buf, k_buf, odd_wanted, first):
     rows = k_buf.shape[0]
     pairs = s_buf.shape[2] // 2
     stats = jnp.zeros((pairs, LANES), jnp.float32)
     weights = []
     for r in range(rows):
-        exponent, stats = soften(s_buf, r, odd_wanted, stats)
+        exponent, stats = soften(s_buf, r, odd_wanted, stats, first)
         weights.append(exponent)
     for r in range(rows):
         weigh(out, weights[r], k_buf, r)
     out[pl.ds(rows * TILES, pairs, stride=rows * TILES + 1), :] = stats
 
 
-def attend_theirs(lengths, queries, cache, theirs, s_buf, k_buf, l_buf, q_buf, arrived):
+def attend_theirs(first, lengths, queries, cache, theirs, s_buf, k_buf, l_buf, q_buf, arrived):
     rows, heads, _ = queries.shape
     shard_len = cache.shape[2]
     me = lax.axis_index("kv")
@@ -91,7 +92,7 @@
             s_buf[r, t] = scores[:, t * LANES : (t + 1) * LANES]
 
     def exponents(r):
-        weights[r], stats[0] = soften(s_buf, r, first_core, stats[0])
+        weights[r], stats[0] = soften(s_buf, r, first_core, stats[0], first)
 
     def numerators(r):
         weigh(theirs, weights[r], k_buf, r)
@@ -110,28 +111,24 @@
     theirs[pl.ds(rows * TILES, heads // 2, stride=rows * TILES + 1), :] = stats[0]
 
 
-def attend_mine(s_buf, k_buf, mine):
-    finish(mine, s_buf, k_buf, lax.rem(lax.axis_index("kv"), 2) == 1)
-
-
-def merge_cores(rows, order, got, mine, merged):
+def attend_mine(first, s_buf, k_buf, mine):
+    finish(mine, s_buf, k_buf, lax.rem(lax.axis_index("kv"), 2) == 1, first)
+
+
+def merge_cores(rows, got, mine, merged):
     sent = rows * TILES + 1
-    chips = len(order)
-    stats = [ref[pl.ds(rows * TILES, chips, stride=sent), :] for ref in (got, mine)]
+    chips = got.shape[0] // sent
+    last = pl.ds(rows * TILES, chips, stride=sent)
+    stats = [got[last, :], mine[last, :]]
     top = jnp.maximum(*stats)
     weights = [jnp.exp(s - top) for s in stats]
     total = sum(pltpu.roll(s, HALF, 1) * w for s, w in zip(stats, weights))
-    both = jnp.where(lane_of(chips) < HALF, top, pltpu.roll(total, HALF, 1))
-    columns = [jnp.transpose(w)[:rows] for w in weights]
-    turned = jnp.concatenate([both[order[0] :], both[: order[0]]], axis=0)
-    merged[pl.ds(rows * TILES, chips, stride=sent), :] = turned
-    for slot, q in enumerate(order):
-        factors = [jnp.broadcast_to(c[:, q : q + 1], (rows, LANES)) for c in columns]
+    merged[last, :] = jnp.where(lane_of(chips) < HALF, top, pltpu.roll(total, HALF, 1))
+    for r in range(rows):
+        columns = [jnp.broadcast_to(w[:, r : r + 1], (chips, LANES)) for w in weights]
         for t in range(TILES):
-            at = pl.ds(q * sent + t * rows, rows)
-            merged[slot * sent + t * rows : slot * sent + (t + 1) * rows, :] = (
-                got[at, :] * factors[0] + mine[at, :] * factors[1]
-            )
+            at = pl.ds(t * rows + r, chips, stride=sent)
+            merged[at, :] = got[at, :] * columns[0] + mine[at, :] * columns[1]
 
 
 def project(rows, order, got, value_up, out_proj, theirs, mine):
@@ -220,7 +217,7 @@
     sent = rows * TILES + 1
     partials = jax.ShapeDtypeStruct((chips * sent, LANES), f32)
     theirs, scores, held = pl.pallas_call(
-        attend_theirs,
+        lambda *refs: attend_theirs(orders[0][0], *refs),
         out_shape=[
             partials,
             jax.ShapeDtypeStruct((rows, shard_len // LANES, heads, LANES), f32),
@@ -237,14 +234,14 @@
     )(*[in_hbm(v) for v in (lengths, queries, latent_cache.transpose(0, 2, 1))])
     got = core_swap(theirs, kv)
     mine = pl.pallas_call(
-        attend_mine,
+        lambda *refs: attend_mine(orders[0][0], *refs),
         out_shape=partials,
         in_specs=vmem_specs(2),
         out_specs=vmem_specs(1)[0],
         compiler_params=params,
     )(scores, held)
     merged = pl.pallas_call(
-        lambda *refs: merge_cores(rows, orders[0], *refs),
+        lambda *refs: merge_cores(rows, *refs),
         out_shape=partials,
         in_specs=vmem_specs(2),
         out_specs=vmem_specs(1)[0],

time: 51.4 us -> 51.3 us (level)
  no operation moved by 1% of the time
where the time goes in v9:
time: 51.3 us; the launch traced here: 51 us
  blocking collectives  36.2 us (71%)
  starting transfers between devices  8.79 us (17%)
  Pallas kernels  5.19 us (10%)
  waiting for transfers between devices  0.77 us (2%)
    all_to_all x1, blocking collectives, on_device(): lax.all_to_all(merged.reshape(chips, 1, sent * LANES), 'kv', 0, 0, axis_i...  20.4 us
    all_to_all x1, blocking collectives, on_device(): lax.all_to_all(summed.reshape(chips, 1, (rows - 1) * LANES), 'kv', 0, 0,...  12.3 us
    ppermute x1, starting transfers between devices, core_swap(): return lax.ppermute(x, 'kv', [(i, i ^ 1) for i in range(kv)])  8.79 us
    all_gather x1, blocking collectives, on_device(): lax.all_gather(theirs, 'kv', axis_index_groups=[[2 * i, 2 * i + 1] for i...  3.59 us
    pallas_call x1, Pallas kernels, on_device(): pl.pallas_call(lambda *refs: attend_theirs(orders[0][0], *refs), out_shap...  2.82 us
  transfers between devices with their start and end apart: 1, of which 1 were waited for; matrix products, arithmetic and copies ran while one was open for 0% of the time, Pallas kernels for 1%

profile of v9, /device:TPU:1, one launch (start us, length us, event | category | flops | bytes accessed | tf_op | source)
XLA Modules:
  0.0 51.0 jit_solution(13906653903418077523)
XLA Ops:
  0.0 2.8 %shard_map.55 = (f32[1056,128]{1,0:T(8,128)S(1)}, f32[8,2,64,128]{3,2,1,0:T(8,128)S(1)}, bf16[8,576,256]{2,1,0:T(8,128)(2,1)S(1)}) custom-call(s32[8]{0:T(128)} %refs_0_.1, bf16[8,64,576]{2,1,0:T(8,128)(2,1)} %refs_1_.2, bf16[8,576,256]{2,1,0:T(8,128)(2,1)} %bitcast.11), custom_call_target="tpu_custom_call" | custom-call | tf_op jit(solution)/shard_map/pallas_call | solution.py:219
  2.8 8.8 %collective-permute-start = (f32[1056,128]{1,0:T(8,128)S(1)}, f32[1056,128]{1,0:T(8,128)S(1)}, u32[]{:S(2)}, u32[]{:S(2)}) collective-permute-start(f32[1056,128]{1,0:T(8,128)S(1)} %get-tuple-element.10), channel_id=1, source_target_pairs={{0,1},{1,0},{2,3},{3,2},{4,5},{5,4},{6,7},{7,6},{8,9},{9,8},{10,11... | collective-permute-start | bytes 1622024 | tf_op jit(solution)/shard_map/ppermute | solution.py:201
  11.6 0.0 copy-start
  11.6 0.0 copy-start.1
  11.7 0.7 %shard_map.56.refs_1_ = f32[1056,128]{1,0:T(8,128)S(1)} custom-call(f32[8,2,64,128]{3,2,1,0:T(8,128)S(1)} %get-tuple-element.11.refs_0_, bf16[8,576,256]{2,1,0:T(8,128)(2,1)S(1)} %get-tuple-element.12.refs_1_), custom_call_target="tpu_custom_call" | custom-call | tf_op jit(solution)/shard_map/pallas_call | solution.py:236
  12.4 0.8 %collective-permute-done.refs_0_ = f32[1056,128]{1,0:T(8,128)S(1)} collective-permute-done((f32[1056,128]{1,0:T(8,128)S(1)}, f32[1056,128]{1,0:T(8,128)S(1)}, u32[]{:S(2)}, u32[]{:S(2)}) %collective-permute-start) | collective-permute-done | bytes 540704 | tf_op jit(solution)/shard_map/ppermute | solution.py:201
  13.2 0.2 shard_map.57
  13.3 20.4 %all_to_all.10 = f32[32,1,4224]{2,1,0:T(1,128)S(1)} all-to-all(f32[32,1,4224]{2,1,0:T(1,128)S(1)} %bitcast.7), channel_id=1, replica_groups={{52,54,56,58,60,62,0,2,4,6,8,10,12,14,16,18,20,22,24,26,28,30,32,34,36,..., dimensions={0} | all-to-all | bytes 1081344 | tf_op jit(solution)/shard_map/all_to_all | solution.py:250
  33.7 0.0 copy-done
  33.7 0.0 copy-done.1
  33.7 0.8 %shard_map.58 = (f32[232,128]{1,0:T(8,128)S(1)}, f32[232,128]{1,0:T(8,128)S(1)}) custom-call(f32[1056,128]{1,0:T(8,128)S(1)} %bitcast.6, bf16[1,512,128]{2,1,0:T(8,128)(2,1)S(1)} %copy-done.1, bf16[128,7168]{1,0:T(8,128)(2,1)S(1)} %copy-done), custom_call_target="tpu_custom_call" | custom-call | tf_op jit(solution)/shard_map/pallas_call | solution.py:255
  34.5 3.6 %all-gather = f32[464,128]{1,0:T(8,128)S(1)} all-gather(f32[232,128]{1,0:T(8,128)S(1)} %get-tuple-element.13), channel_id=2, replica_groups={{0,1},{2,3},{4,5},{6,7},{8,9},{10,11},{12,13},{14,15},{16,17},{18,19},{..., dimensions={0}, use_global_device_ids=true | all-gather | bytes 356352 | tf_op jit(solution)/shard_map/all_gather | solution.py:262
  38.1 12.3 %all_to_all.11 = f32[32,1,896]{2,1,0:T(1,128)S(1)} all-to-all(f32[32,1,896]{2,1,0:T(1,128)S(1)} %bitcast.9), channel_id=1, replica_groups={{38,40,42,44,46,48,50,52,54,56,58,60,62,0,2,4,6,8,10,12,14,16,18,20,22,..., dimensions={0} | all-to-all | bytes 229376 | tf_op jit(solution)/shard_map/all_to_all | solution.py:272
  50.4 0.7 %shard_map.60 = bf16[8,112]{1,0:T(8,128)(2,1)} custom-call(f32[224,128]{1,0:T(8,128)S(1)} %bitcast.10), custom_call_target="tpu_custom_call" | custom-call | tf_op jit(solution)/shard_map/pallas_call | solution.py:275
  (1 shorter events, 0.0 us)
Async XLA Ops:
  2.8 10.3 %collective-permute-start = (f32[1056,128]{1,0:T(8,128)S(1)}, f32[1056,128]{1,0:T(8,128)S(1)}, u32[]{:S(2)}, u32[]{:S(2)}) collective-permute-start(f32[1056,128]{1,0:T(8,128)S(1)} %get-tuple-element.10), channel_id=1, source_target_pairs={{0,1},{1,0},{2,3},{3,2},{4,5},{5,4},{6,7},{7,6},{8,9},{9,8},{10,11... | collective-permute-start | bytes 1622024 | tf_op jit(solution)/shard_map/ppermute | solution.py:201
  11.6 22.1 %copy-start = (bf16[128,7168]{1,0:T(8,128)(2,1)S(1)}, bf16[128,7168]{1,0:T(8,128)(2,1)}, u32[]{:S(2)}) copy-start(bf16[128,7168]{1,0:T(8,128)(2,1)} %refs_2_.1) | copy-start | bytes 5505028
  11.6 22.1 %copy-start.1 = (bf16[1,512,128]{2,1,0:T(8,128)(2,1)S(1)}, bf16[1,512,128]{2,1,0:T(8,128)(2,1)}, u32[]{:S(2)}) copy-start(bf16[1,512,128]{2,1,0:T(8,128)(2,1)} %refs_1_.3) | copy-start | bytes 393220

commit v10 on v8

--- a/solution.py
+++ b/solution.py
@@ -212,7 +212,9 @@
     rows, heads, width = queries.shape
     shard_len = latent_cache.shape[1]
     chips = kv // 2
-    orders = [chips_from(first, chips) for first in (26, 19)]
+    columns, down = 4, chips // 4
+    blocks = [((2 - i) % columns) * down + (3 + j) % down for i in range(columns) for j in range(down)]
+    orders = [chips_from(26, chips), blocks]
     same_core = [[[2 * i + c for i in order] for c in range(2)] for order in orders]
     params = pltpu.CompilerParams(vmem_limit_bytes=8 * 2**20)
     f32 = jnp.float32

time: 51.4 us -> 51.3 us (level)
  no operation moved by 1% of the time
where the time goes in v10:
time: 51.3 us; the launch traced here: 51.1 us
  blocking collectives  36.1 us (70%)
  starting transfers between devices  8.79 us (17%)
  Pallas kernels  5.3 us (10%)
  waiting for transfers between devices  0.77 us (2%)
    all_to_all x1, blocking collectives, on_device(): lax.all_to_all(merged.reshape(chips, 1, sent * LANES), 'kv', 0, 0, axis_i...  20.4 us
    all_to_all x1, blocking collectives, on_device(): lax.all_to_all(summed.reshape(chips, 1, (rows - 1) * LANES), 'kv', 0, 0,...  12.2 us
    ppermute x1, starting transfers between devices, core_swap(): return lax.ppermute(x, 'kv', [(i, i ^ 1) for i in range(kv)])  8.79 us
    all_gather x1, blocking collectives, on_device(): lax.all_gather(theirs, 'kv', axis_index_groups=[[2 * i, 2 * i + 1] for i...  3.59 us
    pallas_call x1, Pallas kernels, on_device(): pl.pallas_call(attend_theirs, out_shape=[partials, jax.ShapeDtypeStruct((...  2.82 us
  transfers between devices with their start and end apart: 1, of which 1 were waited for; matrix products, arithmetic and copies ran while one was open for 0% of the time, Pallas kernels for 1%

profile of v10, /device:TPU:1, one launch (start us, length us, event | category | flops | bytes accessed | tf_op | source)
XLA Modules:
  0.0 51.1 jit_solution(13736428425302294835)
XLA Ops:
  0.0 2.8 %shard_map.55 = (f32[1056,128]{1,0:T(8,128)S(1)}, f32[8,2,64,128]{3,2,1,0:T(8,128)S(1)}, bf16[8,576,256]{2,1,0:T(8,128)(2,1)S(1)}) custom-call(s32[8]{0:T(128)} %lengths.1, bf16[8,64,576]{2,1,0:T(8,128)(2,1)} %queries.1, bf16[8,576,256]{2,1,0:T(8,128)(2,1)} %bitcast.11), custom_call_target="tpu_custom_call" | custom-call | tf_op jit(solution)/shard_map/pallas_call | solution.py:224
  2.8 8.8 %collective-permute-start = (f32[1056,128]{1,0:T(8,128)S(1)}, f32[1056,128]{1,0:T(8,128)S(1)}, u32[]{:S(2)}, u32[]{:S(2)}) collective-permute-start(f32[1056,128]{1,0:T(8,128)S(1)} %get-tuple-element.10), channel_id=1, source_target_pairs={{0,1},{1,0},{2,3},{3,2},{4,5},{5,4},{6,7},{7,6},{8,9},{9,8},{10,11... | collective-permute-start | bytes 1622024 | tf_op jit(solution)/shard_map/ppermute | solution.py:204
  11.6 0.0 copy-start
  11.6 0.0 copy-start.1
  11.7 0.7 %shard_map.56.refs_1_ = f32[1056,128]{1,0:T(8,128)S(1)} custom-call(f32[8,2,64,128]{3,2,1,0:T(8,128)S(1)} %get-tuple-element.11.s_buf, bf16[8,576,256]{2,1,0:T(8,128)(2,1)S(1)} %get-tuple-element.12.k_buf), custom_call_target="tpu_custom_call" | custom-call | tf_op jit(solution)/shard_map/pallas_call | solution.py:241
  12.4 0.8 %collective-permute-done.refs_0_ = f32[1056,128]{1,0:T(8,128)S(1)} collective-permute-done((f32[1056,128]{1,0:T(8,128)S(1)}, f32[1056,128]{1,0:T(8,128)S(1)}, u32[]{:S(2)}, u32[]{:S(2)}) %collective-permute-start) | collective-permute-done | bytes 540704 | tf_op jit(solution)/shard_map/ppermute | solution.py:204
  13.2 0.3 shard_map.57
  13.4 20.4 %all_to_all.10 = f32[32,1,4224]{2,1,0:T(1,128)S(1)} all-to-all(f32[32,1,4224]{2,1,0:T(1,128)S(1)} %bitcast.7), channel_id=1, replica_groups={{52,54,56,58,60,62,0,2,4,6,8,10,12,14,16,18,20,22,24,26,28,30,32,34,36,..., dimensions={0} | all-to-all | bytes 1081344 | tf_op jit(solution)/shard_map/all_to_all | solution.py:255
  33.8 0.0 copy-done
  33.8 0.0 copy-done.1
  33.8 0.8 %shard_map.58 = (f32[232,128]{1,0:T(8,128)S(1)}, f32[232,128]{1,0:T(8,128)S(1)}) custom-call(f32[1056,128]{1,0:T(8,128)S(1)} %bitcast.6, bf16[1,512,128]{2,1,0:T(8,128)(2,1)S(1)} %copy-done.1, bf16[128,7168]{1,0:T(8,128)(2,1)S(1)} %copy-done), custom_call_target="tpu_custom_call" | custom-call | tf_op jit(solution)/shard_map/pallas_call | solution.py:260
  34.6 3.6 %all-gather = f32[464,128]{1,0:T(8,128)S(1)} all-gather(f32[232,128]{1,0:T(8,128)S(1)} %get-tuple-element.13), channel_id=2, replica_groups={{0,1},{2,3},{4,5},{6,7},{8,9},{10,11},{12,13},{14,15},{16,17},{18,19},{..., dimensions={0}, use_global_device_ids=true | all-gather | bytes 356352 | tf_op jit(solution)/shard_map/all_gather | solution.py:267
  38.2 12.2 %all_to_all.11 = f32[32,1,896]{2,1,0:T(1,128)S(1)} all-to-all(f32[32,1,896]{2,1,0:T(1,128)S(1)} %bitcast.9), channel_id=1, replica_groups={{38,40,42,44,46,32,34,36,22,24,26,28,30,16,18,20,6,8,10,12,14,0,2,4,54,..., dimensions={0} | all-to-all | bytes 229376 | tf_op jit(solution)/shard_map/all_to_all | solution.py:277
  50.4 0.7 %shard_map.60 = bf16[8,112]{1,0:T(8,128)(2,1)} custom-call(f32[224,128]{1,0:T(8,128)S(1)} %bitcast.10), custom_call_target="tpu_custom_call" | custom-call | tf_op jit(solution)/shard_map/pallas_call | solution.py:280
  (1 shorter events, 0.0 us)
Async XLA Ops:
  2.8 10.3 %collective-permute-start = (f32[1056,128]{1,0:T(8,128)S(1)}, f32[1056,128]{1,0:T(8,128)S(1)}, u32[]{:S(2)}, u32[]{:S(2)}) collective-permute-start(f32[1056,128]{1,0:T(8,128)S(1)} %get-tuple-element.10), channel_id=1, source_target_pairs={{0,1},{1,0},{2,3},{3,2},{4,5},{5,4},{6,7},{7,6},{8,9},{9,8},{10,11... | collective-permute-start | bytes 1622024 | tf_op jit(solution)/shard_map/ppermute | solution.py:204
  11.6 22.2 %copy-start = (bf16[128,7168]{1,0:T(8,128)(2,1)S(1)}, bf16[128,7168]{1,0:T(8,128)(2,1)}, u32[]{:S(2)}) copy-start(bf16[128,7168]{1,0:T(8,128)(2,1)} %refs_2_.1) | copy-start | bytes 5505028
  11.6 22.2 %copy-start.1 = (bf16[1,512,128]{2,1,0:T(8,128)(2,1)S(1)}, bf16[1,512,128]{2,1,0:T(8,128)(2,1)}, u32[]{:S(2)}) copy-start(bf16[1,512,128]{2,1,0:T(8,128)(2,1)} %refs_1_.1) | copy-start | bytes 393220
